TPU v7x, 128 devices: a whole 4x4x4 slice. The times are simulated.
128 devices in a mesh: section: 2 (over core), seq: 16 (over y, x), wshard: 4 (over z).
Axes of the slice: x: 4, y: 4, z: 4, core: 2. Of those that a mesh axis runs over, the one named last changes fastest.
Arguments:
- inputs: float32 [2, 4, 2048, 1024], P(None, 'wshard', 'seq'), may hold values from -6 to 6
- cotangent: float32 [2, 4, 2048, 1024], P(None, 'wshard', 'seq'), may hold values from -6 to 6
- segments: int32 [2, 4, 2048], P(None, 'wshard'), may hold values from 0 to 8, as said below
- norm_gains: float32 [2, 2, 1024], P('section'), may hold values from 0.5 to 1.5
- attend_in: bfloat16 [2, 1024, 3072], P('section', 'wshard'), may hold values from -0.1875 to 0.1875
- attend_out: bfloat16 [2, 1024, 1024], P('section', 'wshard'), may hold values from -2 to 2
- hidden_in: bfloat16 [2, 1024, 5248], P('section', 'wshard'), may hold values from -0.1875 to 0.1875
- hidden_out: bfloat16 [2, 2624, 1024], P('section', 'wshard'), may hold values from -0.125 to 0.125
Outputs:
- section_outputs: float32 [2, 2, 4, 2048, 1024], P('section', None, 'wshard', 'seq')
- section_input_grads: float32 [2, 2, 4, 2048, 1024], P('section', None, 'wshard', 'seq')
- attend_in_grad: float32 [2, 1024, 3072], P('section', ('seq', 'wshard'))
- attend_out_grad: float32 [2, 1024, 1024], P('section', ('seq', 'wshard'))
- hidden_in_grad: float32 [2, 1024, 5248], P('section', ('seq', 'wshard'))
- hidden_out_grad: float32 [2, 2624, 1024], P('section', ('seq', 'wshard'))
- gain_grads: float32 [2, 2, 1024], P('section', None, ('seq', 'wshard'))
Inputs may be any that keep to these rules, and one draw needn't show every extreme that they name: Segment numbers start at 0 at the start of each sequence, never fall along it and rise by at most one from token to token; a sequence holds at most 9 segments.
All inputs are finite; a program needn't handle non-finite values.
Results may differ from a plain program's by a relative error of at most 0.025.
Values may be sent and summed in bfloat16 or wider, within the bound.
No kernel may reach another device: no remote copies, remote signals or barrier semaphores. Data moves between devices by JAX's collectives and lax.ppermute only.
A program may use at most 192 MiB of HBM per device.

v0:
```python
import functools
import math

import jax
import jax.numpy as jnp
from jax import lax
from jax.experimental import pallas as pl
from jax.experimental.pallas import tpu as pltpu
from jax.sharding import PartitionSpec as P

HEADS = 16
HEAD_DIM = 64
FF = 2624
HALO = 64
FF_PAD = 2688
SEQ_DEV = 16
W_DEV = 4
PAD_ROWS = 48
HIDDEN_BLOCK = 896
QKV_BLOCK = 768

norm_eps = 1e-05
root_half = 1.0 / math.sqrt(2.0)
root_two_pi = 1.0 / math.sqrt(2.0 * math.pi)
score_scale = 1.0 / math.sqrt(HEAD_DIM)

SWAP = [(0, 1), (1, 0)]


def swapped(array):
    return lax.ppermute(array, "section", SWAP)


def norm_parts(rows_in):
    centred = rows_in - jnp.mean(rows_in, axis=1, keepdims=True)
    factor = lax.rsqrt(jnp.mean(centred * centred, axis=1, keepdims=True) + norm_eps)
    return (centred * factor, factor)


def norm_back(grad_norm, normed, factor):
    inner = jnp.mean(grad_norm, axis=1, keepdims=True)
    along = jnp.mean(grad_norm * normed, axis=1, keepdims=True)
    return factor * (grad_norm - inner - normed * along)


def matmul(left, right):
    return jnp.dot(left, right, preferred_element_type=jnp.float32)


def matmul_t(left, right):
    return lax.dot_general(
        left, right, (((1,), (1,)), ((), ())), preferred_element_type=jnp.float32
    )


def inner_rows(left, right):
    return lax.dot_general(
        left, right, (((0,), (0,)), ((), ())), preferred_element_type=jnp.float32
    )


def column_halves(array, on_first):
    even = jnp.concatenate([array[:, 256 * k : 256 * k + 128] for k in range(4)], axis=1)
    odd = jnp.concatenate([array[:, 256 * k + 128 : 256 * k + 256] for k in range(4)], axis=1)
    return (jnp.where(on_first, even, odd), jnp.where(on_first, odd, even))


def from_halves(own, other, on_first):
    even = jnp.where(on_first, own, other)
    odd = jnp.where(on_first, other, own)
    parts = []
    for k in range(4):
        parts += [even[:, 128 * k : 128 * k + 128], odd[:, 128 * k : 128 * k + 128]]
    return jnp.concatenate(parts, axis=1)


def window_allowed(query_seg, key_seg):
    rows, keys = (query_seg.shape[0], key_seg.shape[1])
    offset = lax.broadcasted_iota(jnp.int32, (rows, keys), 1) - lax.broadcasted_iota(
        jnp.int32, (rows, keys), 0
    )
    return (offset >= 0) & (offset <= 2 * HALO) & (query_seg == key_seg)


def attend_kernel(query_seg, key_seg, qkv, mixed, log_total):
    allowed = window_allowed(query_seg[...], key_seg[...])
    width = HEADS * HEAD_DIM
    rows = mixed.shape[0]
    for head in range(HEADS):
        at = head * HEAD_DIM
        q = qkv[HALO : HALO + rows, at : at + HEAD_DIM]
        k = qkv[:, width + at : width + at + HEAD_DIM]
        v = qkv[:, 2 * width + at : 2 * width + at + HEAD_DIM]
        scores = jnp.where(allowed, matmul_t(q, k) * score_scale, -1e30)
        row_max = jnp.max(scores, axis=1, keepdims=True)
        exponent = jnp.exp(scores - row_max)
        total = jnp.sum(exponent, axis=1, keepdims=True)
        probs = (exponent * (1.0 / total)).astype(jnp.bfloat16)
        mixed[:, at : at + HEAD_DIM] = matmul(probs, v).astype(jnp.bfloat16)
        log_total[:, at : at + HEAD_DIM] = jnp.broadcast_to(
            row_max + jnp.log(total), (rows, HEAD_DIM)
        )


def attend_back_kernel(query_seg, key_seg, qkv, log_total, grad_mixed, *refs):
    grad_query, own, before, after = refs[-4:]
    allowed = window_allowed(query_seg[...], key_seg[...])
    width = HEADS * HEAD_DIM
    rows = grad_mixed.shape[0]
    for head in range(HEADS):
        at = head * HEAD_DIM
        q = qkv[HALO : HALO + rows, at : at + HEAD_DIM]
        k = qkv[:, width + at : width + at + HEAD_DIM]
        v = qkv[:, 2 * width + at : 2 * width + at + HEAD_DIM]
        grad = grad_mixed[:, at : at + HEAD_DIM]
        scores = jnp.where(allowed, matmul_t(q, k) * score_scale, -1e30)
        probs = jnp.exp(scores - log_total[:, at : at + 1])
        grad_probs = matmul_t(grad, v)
        inner = jnp.sum(probs * grad_probs, axis=1, keepdims=True)
        grad_scores = (probs * (grad_probs - inner)).astype(jnp.bfloat16)
        grad_query[:, at : at + HEAD_DIM] = (matmul(grad_scores, k) * score_scale).astype(
            jnp.bfloat16
        )
        for place, piece in (
            (at, inner_rows(grad_scores, q) * score_scale),
            (width + at, inner_rows(probs.astype(jnp.bfloat16), grad)),
        ):
            columns = slice(place, place + HEAD_DIM)
            before[:, columns] = piece[:HALO].astype(jnp.bfloat16)
            own[:, columns] = piece[HALO : HALO + rows]
            after[:, columns] = piece[HALO + rows :].astype(jnp.bfloat16)


params = pltpu.CompilerParams(vmem_limit_bytes=40 * 1024 * 1024)


def attend(query_seg, key_seg, qkv):
    rows, width = (query_seg.shape[0], HEADS * HEAD_DIM)
    return pl.pallas_call(
        attend_kernel,
        out_shape=(
            jax.ShapeDtypeStruct((rows, width), jnp.bfloat16),
            jax.ShapeDtypeStruct((rows, width), jnp.float32),
        ),
        compiler_params=params,
        name="attend",
    )(query_seg, key_seg, qkv)


def attend_back(query_seg, key_seg, qkv, log_total, grad_mixed, ready):
    rows, width = (query_seg.shape[0], HEADS * HEAD_DIM)
    return pl.pallas_call(
        attend_back_kernel,
        out_shape=(
            jax.ShapeDtypeStruct((rows, width), jnp.bfloat16),
            jax.ShapeDtypeStruct((rows, 2 * width), jnp.float32),
            jax.ShapeDtypeStruct((HALO, 2 * width), jnp.bfloat16),
            jax.ShapeDtypeStruct((HALO, 2 * width), jnp.bfloat16),
        ),
        in_specs=[pl.BlockSpec(memory_space=pltpu.VMEM)] * 5
        + [pl.BlockSpec(memory_space=pl.ANY)] * len(ready),
        compiler_params=params,
        name="attend_back",
    )(query_seg, key_seg, qkv, log_total, grad_mixed, *ready)


def to_next(array):
    return lax.ppermute(array, "seq", [(i, i + 1) for i in range(SEQ_DEV - 1)])


def to_previous(array):
    return lax.ppermute(array, "seq", [(i + 1, i) for i in range(SEQ_DEV - 1)])


def split_normal(gate):
    cumulative = 0.5 * (1.0 + lax.erf(gate * root_half))
    return cumulative


def grid_call(kernel, name, scalars, grid, in_specs, out_specs, out_shape, scratch, args, aliases=None):
    return pl.pallas_call(
        kernel,
        grid_spec=pltpu.PrefetchScalarGridSpec(
            num_scalar_prefetch=len(scalars),
            grid=grid,
            in_specs=in_specs,
            out_specs=out_specs,
            scratch_shapes=scratch,
        ),
        out_shape=out_shape,
        input_output_aliases=aliases or {},
        compiler_params=params,
        name=name,
    )(*scalars, *args)


def whole(array):
    return pl.BlockSpec(array.shape, lambda n, *_: (0,) * array.ndim)


def columns_at(rows, block, first):
    return pl.BlockSpec((rows, block), lambda n, *_: (0, first + n))


def rows_at(block, columns):
    return pl.BlockSpec((block, columns), lambda n, *_: (n, 0))


def add_to(step, total, value):
    @pl.when(step == 0)
    def _():
        total[...] = value

    @pl.when(step > 0)
    def _():
        total[...] += value


def store_halves(out, own, other, on_first):
    for k in range(4):
        block = slice(128 * k, 128 * k + 128)
        out[:, 256 * k : 256 * k + 128] = jnp.where(on_first, own[:, block], other[:, block])
        out[:, 256 * k + 128 : 256 * k + 256] = jnp.where(on_first, other[:, block], own[:, block])


def qkv_kernel(own, other, weight_own, weight_other, out):
    out[...] = (
        matmul(own[...], weight_own[...]) + matmul(other[...], weight_other[...])
    ).astype(jnp.bfloat16)


def qkv_of(own, other, weights):
    (w_own, at_own), (w_other, at_other) = weights["qkv"]
    width = 3 * HEADS * HEAD_DIM
    depth = own.shape[1]
    return grid_call(
        qkv_kernel,
        "qkv",
        (),
        (width // QKV_BLOCK,),
        [
            whole(own),
            whole(other),
            columns_at(depth, QKV_BLOCK, at_own // QKV_BLOCK),
            columns_at(depth, QKV_BLOCK, at_other // QKV_BLOCK),
        ],
        columns_at(own.shape[0], QKV_BLOCK, 0),
        jax.ShapeDtypeStruct((own.shape[0], width), jnp.bfloat16),
        [],
        (own, other, w_own, w_other),
    )


def qkv_back_kernel(first, grad, weight_own, weight_other, *refs):
    out, total_own, total_other = refs[-3:]
    step = pl.program_id(0)
    add_to(step, total_own, matmul_t(grad[...], weight_own[...]))
    add_to(step, total_other, matmul_t(grad[...], weight_other[...]))

    @pl.when(step == pl.num_programs(0) - 1)
    def _():
        store_halves(out, total_own[...], total_other[...], first[0] == 1)


def qkv_back(first, grad, weights, ready):
    (w_own, at_own), (w_other, at_other) = weights["qkv"]
    rows, width = grad.shape
    depth = w_own.shape[0]
    return grid_call(
        qkv_back_kernel,
        "qkv_back",
        (first,),
        (width // QKV_BLOCK,),
        [
            columns_at(rows, QKV_BLOCK, 0),
            columns_at(depth, QKV_BLOCK, at_own // QKV_BLOCK),
            columns_at(depth, QKV_BLOCK, at_other // QKV_BLOCK),
            *[pl.BlockSpec(memory_space=pl.ANY)] * len(ready),
        ],
        pl.BlockSpec((rows, 2 * depth), lambda n, *_: (0, 0)),
        jax.ShapeDtypeStruct((rows, 2 * depth), jnp.float32),
        [pltpu.VMEM((rows, depth), jnp.float32)] * 2,
        (grad, w_own, w_other, *ready),
    )


def hidden_kernel(
    first, own, other, gate_own, gate_other, up_own, up_other, down_own, down_other, middle,
    gate_out, up_out, product_out, out, total_own, total_other,
):
    step = pl.program_id(0)
    gate = matmul(own[...], gate_own[...]) + matmul(other[...], gate_other[...])
    up = matmul(own[...], up_own[...]) + matmul(other[...], up_other[...])
    product = (gate * split_normal(gate) * up).astype(jnp.bfloat16)
    gate_out[...] = gate
    up_out[...] = up
    product_out[...] = product
    add_to(step, total_own, matmul(product, down_own[...]))
    add_to(step, total_other, matmul(product, down_other[...]))

    @pl.when(step == pl.num_programs(0) - 1)
    def _():
        half = total_own.shape[1]
        mine, theirs, on_first = (total_own[...], total_other[...], first[0] == 1)
        out[:, :half] = middle[:, :half] + jnp.where(on_first, mine, theirs)
        out[:, half:] = middle[:, half:] + jnp.where(on_first, theirs, mine)


def hidden_specs(weights, depth):
    specs, arrays = ([], [])
    for part in ("gate", "up"):
        for array, at in weights[part]:
            specs.append(columns_at(depth, HIDDEN_BLOCK, at // HIDDEN_BLOCK))
            arrays.append(array)
    for array in weights["down"]:
        specs.append(rows_at(HIDDEN_BLOCK, array.shape[1]))
        arrays.append(array)
    return (specs, arrays)


def hidden_forward(first, own, other, middle, weights):
    rows, depth = own.shape
    width = middle.shape[1]
    specs, arrays = hidden_specs(weights, depth)
    piece = columns_at(rows, HIDDEN_BLOCK, 0)
    return grid_call(
        hidden_kernel,
        "hidden",
        (first,),
        (FF_PAD // HIDDEN_BLOCK,),
        [whole(own), whole(other), *specs, whole(middle)],
        (piece, piece, piece, whole(middle)),
        (
            jax.ShapeDtypeStruct((rows, FF_PAD), jnp.float32),
            jax.ShapeDtypeStruct((rows, FF_PAD), jnp.float32),
            jax.ShapeDtypeStruct((rows, FF_PAD), jnp.bfloat16),
            jax.ShapeDtypeStruct((rows, width), jnp.float32),
        ),
        [pltpu.VMEM((rows, width // 2), jnp.float32)] * 2,
        (own, other, *arrays, middle),
    )


def hidden_back_kernel(
    first, grad_own, grad_other, gate_in, up_in, gate_own, gate_other, up_own, up_other, down_own,
    down_other, grad_gate_out, grad_up_out, out, total_own, total_other,
):
    step = pl.program_id(0)
    gate, up = (gate_in[...], up_in[...])
    grad_product = matmul_t(grad_own[...], down_own[...]) + matmul_t(
        grad_other[...], down_other[...]
    )
    cumulative = split_normal(gate)
    derivative = cumulative + gate * jnp.exp(-0.5 * gate * gate) * root_two_pi
    grad_gate = (grad_product * up * derivative).astype(jnp.bfloat16)
    grad_up = (grad_product * gate * cumulative).astype(jnp.bfloat16)
    grad_gate_out[...] = grad_gate
    grad_up_out[...] = grad_up
    add_to(step, total_own, matmul_t(grad_gate, gate_own[...]) + matmul_t(grad_up, up_own[...]))
    add_to(
        step, total_other, matmul_t(grad_gate, gate_other[...]) + matmul_t(grad_up, up_other[...])
    )

    @pl.when(step == pl.num_programs(0) - 1)
    def _():
        store_halves(out, total_own[...], total_other[...], first[0] == 1)


def hidden_back(first, grad_own, grad_other, gate, up, weights):
    rows, half = grad_own.shape
    depth = half
    specs, arrays = hidden_specs(weights, depth)
    piece = columns_at(rows, HIDDEN_BLOCK, 0)
    return grid_call(
        hidden_back_kernel,
        "hidden_back",
        (first,),
        (FF_PAD // HIDDEN_BLOCK,),
        [whole(grad_own), whole(grad_other), piece, piece, *specs],
        (piece, piece, pl.BlockSpec((rows, 2 * depth), lambda n, *_: (0, 0))),
        (
            jax.ShapeDtypeStruct((rows, FF_PAD), jnp.bfloat16),
            jax.ShapeDtypeStruct((rows, FF_PAD), jnp.bfloat16),
            jax.ShapeDtypeStruct((rows, 2 * depth), jnp.float32),
        ),
        [pltpu.VMEM((rows, depth), jnp.float32)] * 2,
        (grad_own, grad_other, gate, up, *arrays),
    )


def attention_input(rows_in, gain):
    normed, factor = norm_parts(rows_in)
    act_in = (normed * gain).astype(jnp.bfloat16)
    before = to_next(act_in[act_in.shape[0] - HALO :])
    after = to_previous(act_in[:HALO])
    return (normed, factor, act_in, jnp.concatenate([before, act_in, after], axis=0))


def layer_forward(rows_in, entry, gain_pair, weights, segs, on_first, first):
    normed1, factor1, act_in, extended = entry
    qkv = qkv_of(*column_halves(extended, on_first), weights)
    mixed, log_total = attend(*segs, qkv)
    own, other = column_halves(mixed, on_first)
    middle = rows_in + matmul(own, weights["out"][0]) + matmul(other, weights["out"][1])
    normed2, factor2 = norm_parts(middle)
    act_mid = (normed2 * gain_pair[1]).astype(jnp.bfloat16)
    own, other = column_halves(act_mid, on_first)
    gate, up, product, output = hidden_forward(first, own, other, middle, weights)
    acts = (jnp.stack([act_in, mixed, act_mid]), product)
    got = tuple(swapped(act) for act in acts)
    kept = (normed1, factor1, qkv, log_total, normed2, factor2, gate, up, acts, got)
    return (output, kept)


def seq_sum(total):
    return lax.psum_scatter(total, "seq", scatter_dimension=0, tiled=True)


ROW_PIECE = FF // (SEQ_DEV * W_DEV)
ROW_GROUPS = PAD_ROWS // 16


def weight_grads(name, items, grads, total, product=None, gains=None, base=None):
    count, width = items[0][0].shape[1:]
    block = 256
    in_specs, args = ([], [])
    for acts, got, member, *_ in items:
        for array in (acts, got):
            in_specs.append(pl.BlockSpec((1, count, block), lambda n, m=member: (m, 0, n)))
            args.append(array)
    for pair in grads:
        in_specs += [whole(array) for array in pair]
        args += list(pair)
    scratch = [pltpu.VMEM((2 * count, pair[0].shape[1]), jnp.bfloat16) for pair in grads]
    if product is not None:
        in_specs += [whole(array) for array in product[:2]]
        args += list(product[:2])
        half = grads[product[2]][0].shape[1] - product[3]
        scratch += [
            pltpu.VMEM((FF_PAD, half), jnp.float32),
            pltpu.VMEM((width, ROW_GROUPS * half), jnp.bfloat16),
        ]
    if gains is not None:
        in_specs.append(rows_at(block, gains[0].shape[1]))
        args.append(gains[0])
    aliases = {}
    columns = total
    if base is not None:
        aliases = {len(args): 0}
        in_specs.append(pl.BlockSpec(memory_space=pl.ANY))
        args.append(base)
        columns = sum(item[5] for item in items)

    def kernel(*refs):
        act_refs = refs[: 2 * len(items)]
        grad_refs = refs[2 * len(items) : 2 * (len(items) + len(grads))]
        rest = refs[2 * (len(items) + len(grads)) : len(args)]
        out, token = refs[len(args) : len(args) + 2]
        rows = refs[len(args) + 2 :]
        step = pl.program_id(0)
        token[...] = jnp.zeros(token.shape, token.dtype)

        @pl.when(step == 0)
        def _():
            for k in range(len(grads)):
                rows[k][:count] = grad_refs[2 * k][...]
                rows[k][count:] = grad_refs[2 * k + 1][...]
            if product is not None:
                down, groups = rows[-2:]
                for at in range(0, FF_PAD, 896):
                    part = jnp.concatenate([r[:, at : at + 896] for r in rest[:2]], axis=0)
                    down[at : at + 896] = inner_rows(part, rows[product[2]][:, product[3] :])
                for piece in range(SEQ_DEV * W_DEV):
                    for group in range(ROW_GROUPS):
                        first_row = piece * ROW_PIECE + group * 16
                        groups[
                            16 * piece : 16 * piece + 16, group * half : (group + 1) * half
                        ] = down[first_row : first_row + 16].astype(jnp.bfloat16)

        for k, (_, _, _, which, at, size, place) in enumerate(items):
            acts = jnp.concatenate([act_refs[2 * k][0], act_refs[2 * k + 1][0]], axis=0)
            for part in range(0, size, 512):
                wide = min(512, size - part)
                out[:, place + part : place + part + wide] = inner_rows(
                    acts, rows[which][:, at + part : at + part + wide]
                ).astype(jnp.bfloat16)
        if product is not None:
            place = product[4]
            out[:, place : place + ROW_GROUPS * half] = rows[-1][
                pl.ds(pl.multiple_of(step * block, block), block)
            ]
        if gains is not None:
            place = gains[1]
            out[:, place : place + gains[0].shape[1]] = rest[2 if product is not None else 0][...]

    return grid_call(
        kernel,
        name,
        (),
        (width // block,),
        in_specs,
        (rows_at(block, columns), pl.BlockSpec((8, 128), lambda n: (0, 0))),
        (
            jax.ShapeDtypeStruct((width, total), jnp.bfloat16),
            jax.ShapeDtypeStruct((8, 128), jnp.float32),
        ),
        scratch,
        args,
        aliases,
    )


def core_halves(pairs, on_first):
    low, high = [jnp.concatenate([p[k] for p in pairs], axis=1) for k in range(2)]
    return (jnp.where(on_first, low, high), swapped(jnp.where(on_first, high, low)))


def layer_backward(grad_out, kept, gain_pair, weights, segs, on_first, first, ready_of, late_of):
    (normed1, factor1, qkv, log_total, normed2, factor2, gate, up, _, _) = kept
    rows, width = normed1.shape
    half = width // 2
    grad_branch = grad_out.astype(jnp.bfloat16)
    low, high = (grad_branch[:, :half], grad_branch[:, half:])
    branch_own, branch_other = (jnp.where(on_first, low, high), jnp.where(on_first, high, low))
    grad_gate, grad_up, grad_norm2 = hidden_back(
        first, branch_own, branch_other, gate, up, weights
    )
    hidden_pair = core_halves(((grad_gate, grad_up), (low, high)), on_first)
    gain_mid = jnp.sum(normed2 * grad_norm2, axis=0)
    grad_middle = grad_out + norm_back(grad_norm2 * gain_pair[1], normed2, factor2)
    grad_attn = grad_middle.astype(jnp.bfloat16)
    mine, theirs = [matmul_t(grad_attn, w) for w in weights["out"]]
    grad_mixed = from_halves(mine, theirs, on_first).astype(jnp.bfloat16)
    grad_query, grad_own, grad_before, grad_after = attend_back(
        *segs, qkv, log_total, grad_mixed, ready_of(hidden_pair)
    )
    from_previous = to_next(grad_after).astype(jnp.float32)
    from_next = to_previous(grad_before).astype(jnp.float32)
    grad_pairs = grad_own + jnp.concatenate([from_previous, from_next], axis=0)
    grad_qkv = jnp.concatenate([grad_query, grad_pairs.astype(jnp.bfloat16)], axis=1)
    attn_pair = core_halves(
        (
            (grad_qkv[:, : 3 * half], grad_qkv[:, 3 * half :]),
            (grad_attn[:, :half], grad_attn[:, half:]),
        ),
        on_first,
    )
    grad_norm1 = qkv_back(first, grad_qkv, weights, late_of(attn_pair))
    gain_first = jnp.sum(normed1 * grad_norm1, axis=0)
    grad_inputs = grad_middle + norm_back(grad_norm1 * gain_pair[0], normed1, factor1)
    gains = jnp.stack([gain_first, gain_mid])
    return (grad_inputs, hidden_pair, attn_pair, gains)


def summed_over_w(block, place):
    rows = block.shape[0] // W_DEV
    total = lax.dynamic_slice_in_dim(block, place * rows, rows).astype(jnp.float32)
    for step in range(1, W_DEV):
        part = lax.dynamic_slice_in_dim(block, lax.rem(place + step, W_DEV) * rows, rows)
        got = lax.ppermute(part, "wshard", [(j, (j + step) % W_DEV) for j in range(W_DEV)])
        total = total + got.astype(jnp.float32)
    return total


def summed_by_steps(block, seq_place, w_place):
    side = 4
    columns = block.shape[1]

    def phase(parts, axis, at, place, route):
        size = parts.shape[at]

        def part(step):
            return lax.dynamic_index_in_dim(parts, lax.rem(place + step, size), at, keepdims=False)

        total = part(0).astype(jnp.float32)
        for step in range(1, size):
            total = total + lax.ppermute(part(step), axis, route(step)).astype(jnp.float32)
        return total

    total = phase(
        block.reshape(SEQ_DEV, W_DEV, 16, columns),
        "wshard",
        1,
        w_place,
        lambda step: [(j, (j + step) % W_DEV) for j in range(W_DEV)],
    )
    total = phase(
        total.astype(jnp.bfloat16).reshape(side, side, 16, columns),
        "seq",
        1,
        lax.rem(seq_place, side),
        lambda step: [
            (side * y + x, side * y + (x + step) % side) for y in range(side) for x in range(side)
        ],
    )
    return phase(
        total.astype(jnp.bfloat16),
        "seq",
        0,
        seq_place // side,
        lambda step: [
            (side * y + x, side * ((y + step) % side) + x) for y in range(side) for x in range(side)
        ],
    )


def per_device(
    inputs, cotangent, segments, norm_gains, attend_in, attend_out, hidden_in, hidden_out
):
    on_first = lax.axis_index("section") == 0
    core = lax.axis_index("section")
    seq_place = lax.axis_index("seq")
    w_place = lax.axis_index("wshard")

    def by_core(first, second):
        return jnp.where(on_first, first, second)

    def sections(own, got):
        return (by_core(own, got), by_core(got, own))

    slice_rows = attend_in.shape[1] // (2 * SEQ_DEV)
    pad = jnp.zeros((slice_rows, FF_PAD - FF), jnp.bfloat16)
    width = inputs.shape[3]

    def row_slice(which):
        at = (which * SEQ_DEV + seq_place) * slice_rows
        hidden, qkv, out = [
            lax.dynamic_slice_in_dim(w[0], at, slice_rows)
            for w in (hidden_in, attend_in, attend_out)
        ]
        return jnp.concatenate([hidden[:, :FF], pad, hidden[:, FF:], pad, qkv, out], axis=1)

    row_pieces = sections(row_slice(core), swapped(row_slice(1 - core)))
    hidden_width, qkv_width = (2 * FF_PAD, 3 * width)
    out_at = hidden_width + qkv_width

    def gathered(piece):
        return lax.all_gather(piece, ("wshard", "seq"), axis=0, tiled=True)

    first_own = gathered(row_pieces[0])
    half = hidden_out.shape[2] // 2
    low, high = (hidden_out[0, :, :half], hidden_out[0, :, half:])
    down_pieces = sections(by_core(low, high), swapped(by_core(high, low)))
    w_up = [(j, (j + 1) % W_DEV) for j in range(W_DEV)]
    w_down = [(j, i) for i, j in w_up]
    gain_pairs = sections(norm_gains[0], swapped(norm_gains[0]))

    def neighbours(piece):
        return (lax.ppermute(piece, "wshard", w_up), lax.ppermute(piece, "wshard", w_down))

    def down_of(piece, below, above):
        far = jnp.concatenate(
            [
                lax.ppermute(below[:, : half // 2], "wshard", w_up),
                lax.ppermute(above[:, half // 2 :], "wshard", w_down),
            ],
            axis=1,
        )
        own = jnp.zeros((FF_PAD, half), jnp.bfloat16)
        for step, part in enumerate((piece, above, far, below)):
            own = lax.dynamic_update_slice_in_dim(
                own, part, lax.rem(w_place + step, W_DEV) * piece.shape[0], 0
            )
        return (own, swapped(own))

    rows_in = by_core(inputs[0, 0], inputs[1, 0])
    row_count = rows_in.shape[0]
    segment_row = by_core(segments[0, 0], segments[1, 0])
    padded = jnp.pad(segment_row, (HALO, HALO), constant_values=-1)
    first_row = seq_place * row_count
    segs = (
        lax.dynamic_slice_in_dim(segment_row, first_row, row_count)[:, None],
        lax.dynamic_slice_in_dim(padded, first_row, row_count + 2 * HALO)[None, :],
    )
    entry = attention_input(rows_in, gain_pairs[0][0])
    row_piece, entry = lax.optimization_barrier((row_pieces[1], entry))
    second_own = gathered(row_piece)
    first_own, down_piece, first_down, entry, gain_pairs, segs = lax.optimization_barrier(
        (first_own, down_pieces[1], down_of(down_pieces[0], *neighbours(down_pieces[0])), entry, gain_pairs, segs)
    )
    near = neighbours(down_piece)

    def weights_of(own, other, qkv_other, out_other, down):
        return {
            "qkv": ((own, hidden_width), qkv_other),
            "gate": ((own, 0), (other, 0)),
            "up": ((own, FF_PAD), (other, FF_PAD)),
            "out": (own[:, out_at:], out_other),
            "down": down,
        }

    first = on_first.astype(jnp.int32)[None]
    other = swapped(first_own)
    first_weights = weights_of(
        first_own, other, (other, hidden_width), other[:, out_at:], first_down
    )
    middle, kept0 = layer_forward(
        rows_in, entry, gain_pairs[0], first_weights, segs, on_first, first
    )
    middle, near = lax.optimization_barrier((middle, near))
    second_own, second_down, entry = lax.optimization_barrier(
        (
            second_own, down_of(down_piece, *near), attention_input(middle, gain_pairs[1][0]),
        )
    )
    qkv_other, out_other, second_own = lax.optimization_barrier(
        (
            swapped(second_own[:, hidden_width:out_at]), swapped(second_own[:, out_at:]),
            second_own,
        )
    )
    weights = (
        first_weights,
        weights_of(second_own, swapped(second_own), (qkv_other, 0), out_other, second_down),
    )
    final, kept1 = layer_forward(middle, entry, gain_pairs[1], weights[1], segs, on_first, first)
    upstream = by_core(cotangent[0, 0], cotangent[1, 0])
    attn_cols, out_cols, down_cols = (qkv_width // 2, half, ROW_GROUPS * half)
    hidden_end = FF_PAD + down_cols
    second_at = attn_cols + out_cols
    side_at = out_cols + down_cols
    hidden_at = second_at + attn_cols
    total = hidden_at + FF_PAD

    def attn_items(kept, which, at):
        acts, got = (kept[-2][0], kept[-1][0])
        return [
            (acts, got, 0, which, 0, attn_cols, at),
            (acts, got, 1, which, attn_cols, out_cols, at + attn_cols),
        ]

    def hidden_items(kept, which, at, down_at):
        acts, got = (kept[-2], kept[-1])
        return (
            [(acts[0], got[0], 2, which, 0, FF_PAD, at)],
            (acts[1], got[1], which, FF_PAD, down_at),
        )

    early_grads = []

    def make_early(hidden_pair):
        items, product = hidden_items(kept1, 0, 0, FF_PAD)
        early_grads.extend(weight_grads("hidden_grads", items, [hidden_pair], hidden_end, product))
        return early_grads[1:]

    grads1, _, attn_pair1, gains1 = layer_backward(
        upstream, kept1, gain_pairs[1], weights[1], segs, on_first, first, make_early, lambda _: ()
    )
    early = seq_sum(early_grads[0])
    late_grads, side_grads = ([], [])

    def make_joint(hidden_pair):
        items, product = hidden_items(kept0, 1, hidden_at, out_cols)
        qkv_item, out_item = attn_items(kept1, 0, 0)
        pairs = [attn_pair1, hidden_pair]
        late_grads.append(
            weight_grads("joint_grads", [qkv_item[:-1] + (second_at,)] + items, pairs, total)[0]
        )
        side_grads.append(
            functools.partial(
                weight_grads, "side_grads", [out_item[:-1] + (0,)], pairs, side_at + 128, product
            )
        )
        return (hidden_pair[1], attn_pair1[1], *kept0[-1])

    def make_late(attn_pair):
        base = late_grads.pop()
        late_grads.extend(
            weight_grads("attn_grads", attn_items(kept0, 0, 0), [attn_pair], total, base=base)
        )
        return late_grads[1:]

    grads0, _, _, gains0 = layer_backward(
        grads1, kept0, gain_pairs[0], weights[0], segs, on_first, first, make_joint, make_late
    )
    late = seq_sum(late_grads[0])
    gains = jnp.concatenate([gains0, gains1], axis=0)
    gains = jnp.pad(gains, ((0, 128 - gains.shape[0]), (0, 0))).T.astype(jnp.bfloat16)
    side = side_grads[0](gains=(gains, side_at))[0]
    side_total = summed_by_steps(side, seq_place, w_place)

    def placed(first, second):
        mine, give = (by_core(first, second), by_core(second, first))
        got = swapped(give)
        return jnp.stack([by_core(mine, got), by_core(got, mine)])[None, :, None]

    section_outputs = placed(middle, final)
    section_input_grads = placed(grads0, grads1)

    early_total, late_total = (summed_over_w(early, w_place), summed_over_w(late, w_place))
    gain_part = side_total[:, side_at:]
    of_first = jnp.concatenate(
        [
            late_total[:, :second_at], gain_part, late_total[:, hidden_at:],
            side_total[:, out_cols:side_at],
        ],
        axis=1,
    )
    of_second = jnp.concatenate(
        [late_total[:, second_at:hidden_at], side_total[:, :out_cols], gain_part, early_total],
        axis=1,
    )
    mine, got = (by_core(of_first, of_second), swapped(by_core(of_second, of_first)))
    low, high = (by_core(mine, got), by_core(got, mine))
    hidden_at = second_at + 128
    qkv_rows = jnp.concatenate([low[:, :attn_cols], high[:, :attn_cols]], axis=1)
    attn_rows = jnp.concatenate([low[:, attn_cols:second_at], high[:, attn_cols:second_at]], axis=1)
    gain_part = (low + high)[:, second_at:hidden_at]
    gain_rows = by_core(gain_part[:, :2], gain_part[:, 2:4]).T
    hidden_rows = jnp.concatenate(
        [low[:, hidden_at : hidden_at + FF], high[:, hidden_at : hidden_at + FF]], axis=1
    )
    down_total = jnp.concatenate(
        [
            jnp.concatenate([h[:, at : at + half] for h in (low, high)], axis=1)
            for at in range(hidden_at + FF_PAD, low.shape[1], half)
        ],
        axis=0,
    )[:ROW_PIECE]
    return (
        section_outputs,
        section_input_grads,
        qkv_rows[None],
        attn_rows[None],
        hidden_rows[None],
        down_total[None],
        gain_rows[None],
    )


def solution(mesh):
    placed = (
        P(None, "wshard", "seq", None),
        P(None, "wshard", "seq", None),
        P(None, "wshard", None),
        P("section", None, None),
        P("section", "wshard", None),
        P("section", "wshard", None),
        P("section", "wshard", None),
        P("section", "wshard", None),
    )
    return jax.shard_map(
        per_device,
        mesh=mesh,
        in_specs=placed,
        out_specs=(
            P("section", None, "wshard", "seq", None),
            P("section", None, "wshard", "seq", None),
            P("section", ("seq", "wshard"), None),
            P("section", ("seq", "wshard"), None),
            P("section", ("seq", "wshard"), None),
            P("section", ("seq", "wshard"), None),
            P("section", None, ("seq", "wshard")),
        ),
        check_vma=False,
    )
```

profile of v0, /device:TPU:1, one launch (start us, length us, event | category | flops | bytes accessed | tf_op | source)
XLA Modules:
  0.0 495.0 jit_solution(15523590224473912635)
XLA Ops:
  18.2 4.0 collective-permute-start.8
  28.2 3.8 collective-permute-start.2
  32.1 14.0 %collective-permute-done.2 = bf16[656,512]{1,0:T(8,128)(2,1)S(1)} collective-permute-done((bf16[656,512]{1,0:T(8,128)(2,1)S(1)}, bf16[656,512]{1,0:T(8,128)(2,1)S(1)}, u32[]{:S(2)}, u32[]{:S(2)}) %collective-permute-start.2) | collective-permute-done | bytes 671776 | tf_op jit(solution)/shard_map/ppermute | solution.py:649
  46.9 3.4 collective-permute-start.5
  53.1 6.2 %collective-permute-done.5 = bf16[656,256]{1,0:T(8,128)(2,1)} collective-permute-done((bf16[656,256]{1,0:T(8,128)(2,1)}, bf16[656,256]{1,0:T(8,128)(2,1)}, u32[]{:S(2)}, u32[]{:S(2)}) %collective-permute-start.5) | collective-permute-done | bytes 335904 | tf_op jit(solution)/shard_map/ppermute | solution.py:655
  59.4 6.2 %collective-permute-done.4 = bf16[656,256]{1,0:T(8,128)(2,1)} collective-permute-done((bf16[656,256]{1,0:T(8,128)(2,1)}, bf16[656,256]{1,0:T(8,128)(2,1)}, u32[]{:S(2)}, u32[]{:S(2)}) %collective-permute-start.4) | collective-permute-done | bytes 335904 | tf_op jit(solution)/shard_map/ppermute | solution.py:654
  68.8 4.7 collective-permute-done.6.down_other
  73.6 27.3 %all-gather.3.cloned.1.call-done.weight_own.gate_own.up_own = bf16[512,9472]{1,0:T(8,128)(2,1)} async-done(((bf16[8,9472]{1,0:T(8,128)(2,1)}), bf16[512,9472]{1,0:T(8,128)(2,1)}) %all-gather.3.cloned.1.call-update) | async-done | bytes 9699344 | tf_op jit(solution)/shard_map/all_gather | solution.py:638
  105.6 10.9 %collective-permute-done.10.weight_other.gate_other.up_other = bf16[512,9472]{1,0:T(8,128)(2,1)} collective-permute-done((bf16[512,9472]{1,0:T(8,128)(2,1)}, bf16[512,9472]{1,0:T(8,128)(2,1)}, u32[]{:S(2)}, u32[]{:S(2)}) %collective-permute-start.10) | collective-permute-done | bytes 9699360 | tf_op jit(solution)/shard_map/ppermute | solution.py:31
  116.5 3.8 copy-done.1
  120.3 4.4 qkv.2
  124.6 2.9 attend.2
  132.2 7.5 %hidden.2 = (f32[128,2688]{1,0:T(8,128)S(1)}, f32[128,2688]{1,0:T(8,128)S(1)}, bf16[128,2688]{1,0:T(8,128)(2,1)S(1)}, f32[128,1024]{1,0:T(8,128)S(1)}) custom-call(s32[1]{0:T(128)} %bitcast.first, bf16[128,512]{1,0:T(8,128)(2,1)S(1)} %get-tuple-element.288.own, bf16[128,512]{1,0:T(8,128)(2,1)S(1)} %get-tuple-element.287.other, ...), custom_call_target="tpu_custom_call" | custom-call | tf_op jit(solution)/shard_map/hidden/pallas_call | solution.py:181
  149.3 3.7 collective-permute-done.14
  153.0 3.1 collective-permute-done.13
  162.9 4.0 collective-permute-start.16
  166.9 4.8 collective-permute-done.17
  172.7 17.4 %all-gather.5.cloned.1.call-done.weight_own.gate_own.up_own = bf16[512,9472]{1,0:T(8,128)(2,1)} async-done(((bf16[8,9472]{1,0:T(8,128)(2,1)}), bf16[512,9472]{1,0:T(8,128)(2,1)}) %all-gather.5.cloned.1.call-update) | async-done | bytes 9699344 | tf_op jit(solution)/shard_map/all_gather | solution.py:638
  194.5 5.3 %collective-permute-done.19 = bf16[512,1024]{1,0:T(8,128)(2,1)S(1)} collective-permute-done((bf16[512,1024]{1,0:T(8,128)(2,1)S(1)}, bf16[512,1024]{1,0:T(8,128)(2,1)S(1)}, u32[]{:S(2)}, u32[]{:S(2)}) %collective-permute-start.19) | collective-permute-done | bytes 1048608 | tf_op jit(solution)/shard_map/ppermute | solution.py:31
  200.6 4.8 qkv.3
  205.5 2.9 attend.3
  211.1 4.0 collective-permute-done.20.gate_other.up_other
  215.1 3.7 copy-done.50
  218.9 8.0 %hidden.3 = (f32[128,2688]{1,0:T(8,128)S(1)}, f32[128,2688]{1,0:T(8,128)S(1)}, bf16[128,2688]{1,0:T(8,128)(2,1)S(1)}, f32[128,1024]{1,0:T(8,128)S(1)}) custom-call(s32[1]{0:T(128)} %bitcast.first, bf16[128,512]{1,0:T(8,128)(2,1)S(1)} %get-tuple-element.268.own, bf16[128,512]{1,0:T(8,128)(2,1)S(1)} %get-tuple-element.267.other, ...), custom_call_target="tpu_custom_call" | custom-call | tf_op jit(solution)/shard_map/hidden/pallas_call | solution.py:181
  227.7 9.6 %hidden_back.2 = (bf16[128,2688]{1,0:T(8,128)(2,1)S(1)}, bf16[128,2688]{1,0:T(8,128)(2,1)S(1)}, f32[128,1024]{1,0:T(8,128)S(1)}) custom-call(s32[1]{0:T(128)} %bitcast.first, bf16[128,512]{1,0:T(8,128)(2,1)S(1)} %get-tuple-element.262.grad_own, bf16[128,512]{1,0:T(8,128)(2,1)S(1)} %get-tuple-element.263.grad_other, ...), custom_call_target="tpu_custom_call" | custom-call | tf_op jit(solution)/shard_map/hidden_back/pallas_call | solution.py:181
  242.9 3.7 hidden_grads.1
  246.7 3.4 copy-done.16
  256.7 5.8 %attend_back.2 = (bf16[128,1024]{1,0:T(8,128)(2,1)S(1)}, f32[128,2048]{1,0:T(8,128)S(1)}, bf16[64,2048]{1,0:T(8,128)(2,1)S(1)}, bf16[64,2048]{1,0:T(8,128)(2,1)S(1)}) custom-call(s32[128,1]{1,0:T(8,128)S(1)} %copy.38.query_seg, s32[1,256]{1,0:T(1,128)S(1)} %bitcast.131, bf16[256,3072]{1,0:T(8,128)(2,1)S(1)} %copy-done.9, f32[128,1024]{1,0:T(8,128)S(1)} %copy-done.47, ...), custom_call_target="tpu_custom_call" | custom-call | tf_op jit(solution)/shard_map/attend_back/pallas_call | solution.py:152
  263.8 4.0 collective-permute-start.25
  269.1 8.8 %collective-permute-done.26 = bf16[64,2048]{1,0:T(8,128)(2,1)S(1)} collective-permute-done((bf16[64,2048]{1,0:T(8,128)(2,1)S(1)}, bf16[64,2048]{1,0:T(8,128)(2,1)S(1)}, u32[]{:S(2)}, u32[]{:S(2)}) %collective-permute-start.26) | collective-permute-done | bytes 262176 | tf_op jit(solution)/shard_map/ppermute | solution.py:172
  278.1 3.9 copy-done
  282.0 4.0 qkv_back.2
  288.1 9.2 %hidden_back.3 = (bf16[128,2688]{1,0:T(8,128)(2,1)S(1)}, bf16[128,2688]{1,0:T(8,128)(2,1)S(1)}, f32[128,1024]{1,0:T(8,128)S(1)}) custom-call(s32[1]{0:T(128)} %bitcast.first, bf16[128,512]{1,0:T(8,128)(2,1)S(1)} %get-tuple-element.256.grad_own, bf16[128,512]{1,0:T(8,128)(2,1)S(1)} %get-tuple-element.257.grad_other, f32[128,2688]{1,0:T(8,128)S(1)} %copy-done.36, ...), custom_call_target="tpu_custom_call" | custom-call | tf_op jit(solution)/shard_map/hidden_back/pallas_call | solution.py:181
  307.7 5.8 %attend_back.3 = (bf16[128,1024]{1,0:T(8,128)(2,1)S(1)}, f32[128,2048]{1,0:T(8,128)S(1)}, bf16[64,2048]{1,0:T(8,128)(2,1)S(1)}, bf16[64,2048]{1,0:T(8,128)(2,1)S(1)}) custom-call(s32[128,1]{1,0:T(8,128)S(1)} %copy.38.query_seg, s32[1,256]{1,0:T(1,128)S(1)} %bitcast.132, bf16[256,3072]{1,0:T(8,128)(2,1)S(1)} %copy-done.11, f32[128,1024]{1,0:T(8,128)S(1)} %copy-done.49, ...), custom_call_target="tpu_custom_call" | custom-call | tf_op jit(solution)/shard_map/attend_back/pallas_call | solution.py:152
  314.8 4.6 collective-permute-start.31
  319.5 4.4 collective-permute-done.32
  329.4 6.3 %joint_grads.1 = (bf16[1024,6272]{1,0:T(8,128)(2,1)}, f32[8,128]{1,0:T(8,128)}) custom-call(bf16[3,128,1024]{2,1,0:T(8,128)(2,1)S(1)} %copy-done.15, bf16[3,128,1024]{2,1,0:T(8,128)(2,1)S(1)} %copy-done.22, bf16[3,128,1024]{2,1,0:T(8,128)(2,1)S(1)} %pad_maximum_fusion.7.refs_2_.refs_0_, ...), custom_call_target="tpu_custom_call" | custom-call | tf_op jit(solution)/shard_map/joint_grads/pallas_call | solution.py:181
  335.7 3.7 attn_grads.1
  340.5 3.8 copy-done.2
  344.3 5.2 %qkv_back.3 = f32[128,1024]{1,0:T(8,128)S(1)} custom-call(s32[1]{0:T(128)} %bitcast.first, bf16[128,3072]{1,0:T(8,128)(2,1)S(1)} %pad_maximum_fusion.1.grad, bf16[512,9472]{1,0:T(8,128)(2,1)S(1)} %copy-done.2, bf16[512,9472]{1,0:T(8,128)(2,1)} %collective-permute-done.10.weight_other.gate_other.up_other, f32[8,128]{1,0:T(8,128)S(1)} %get-tuple-element.126.refs_0_), custom_call_target="tpu_custom_call" | custom-call | tf_op jit(solution)/shard_map/qkv_back/pallas_call | solution.py:181
  371.5 17.4 %collective-permute-done.40 = bf16[16,16,2176]{2,1,0:T(8,128)(2,1)} collective-permute-done((bf16[16,16,2176]{2,1,0:T(8,128)(2,1)}, bf16[16,16,2176]{2,1,0:T(8,128)(2,1)}, u32[]{:S(2)}, u32[]{:S(2)}) %collective-permute-start.40) | collective-permute-done | bytes 1114144 | tf_op jit(solution)/shard_map/ppermute | solution.py:577
  388.9 2.9 collective-permute-done.39
  391.8 25.8 %collective-permute-done.38 = bf16[16,16,2176]{2,1,0:T(8,128)(2,1)} collective-permute-done((bf16[16,16,2176]{2,1,0:T(8,128)(2,1)}, bf16[16,16,2176]{2,1,0:T(8,128)(2,1)}, u32[]{:S(2)}, u32[]{:S(2)}) %collective-permute-start.38) | collective-permute-done | bytes 1114144 | tf_op jit(solution)/shard_map/ppermute | solution.py:577
  420.5 8.3 %collective-permute-start.43 = (bf16[4,16,2176]{2,1,0:T(8,128)(2,1)S(1)}, bf16[4,16,2176]{2,1,0:T(8,128)(2,1)S(1)}, u32[]{:S(2)}, u32[]{:S(2)}) collective-permute-start(bf16[4,16,2176]{2,1,0:T(8,128)(2,1)S(1)} %get-tuple-element.200), channel_id=1, source_target_pairs={{0,12},{4,0},{8,4},{12,8},{16,28},{20,16},{24,20},{28,24},{32,44},... | collective-permute-start | bytes 835592 | tf_op jit(solution)/shard_map/ppermute | solution.py:577
  429.5 15.5 %collective-permute-done.43 = bf16[4,16,2176]{2,1,0:T(8,128)(2,1)S(1)} collective-permute-done((bf16[4,16,2176]{2,1,0:T(8,128)(2,1)S(1)}, bf16[4,16,2176]{2,1,0:T(8,128)(2,1)S(1)}, u32[]{:S(2)}, u32[]{:S(2)}) %collective-permute-start.43) | collective-permute-done | bytes 278560 | tf_op jit(solution)/shard_map/ppermute | solution.py:577
  445.0 4.7 collective-permute-done.41
  449.9 4.5 collective-permute-start.46
  474.7 4.5 collective-permute-done.35
  (403 shorter events, 148.5 us)
Async XLA Ops:
  7.2 93.6 %all-gather.3.cloned.1.call-start = ((), (), s32[]{:S(2)}) async-start(), calls=%async_computation.2 | async-start | bytes 9850880 | tf_op jit(solution)/shard_map/all_gather | solution.py:638
  13.3 176.8 %all-gather.5.cloned.1.call-start = ((), (), s32[]{:S(2)}) async-start(), calls=%async_computation.3 | async-start | bytes 9850880 | tf_op jit(solution)/shard_map/all_gather | solution.py:638
  14.8 10.5 %collective-permute-start.1 = (bf16[656,512]{1,0:T(8,128)(2,1)}, bf16[656,512]{1,0:T(8,128)(2,1)}, u32[]{:S(2)}, u32[]{:S(2)}) collective-permute-start(bf16[656,512]{1,0:T(8,128)(2,1)} %select_bitcast_fusion), channel_id=1, source_target_pairs={{0,64},{64,0},{1,65},{65,1},{2,66},{66,2},{3,67},{67,3},{4,68},{68... | collective-permute-start | bytes 2015240 | tf_op jit(solution)/shard_map/ppermute | solution.py:31
  16.9 6.6 %collective-permute-start.9 = (bf16[64,1024]{1,0:T(8,128)(2,1)S(1)}, bf16[64,1024]{1,0:T(8,128)(2,1)S(1)}, u32[]{:S(2)}, u32[]{:S(2)}) collective-permute-start(bf16[64,1024]{1,0:T(8,128)(2,1)S(1)} %get-tuple-element.306), channel_id=1, source_target_pairs={{4,0},{8,4},{12,8},{16,12},{20,16},{24,20},{28,24},{32,28},{36,32}... | collective-permute-start | bytes 393224 | tf_op jit(solution)/shard_map/ppermute | solution.py:172
  18.2 6.2 %collective-permute-start.8 = (bf16[64,1024]{1,0:T(8,128)(2,1)S(1)}, bf16[64,1024]{1,0:T(8,128)(2,1)S(1)}, u32[]{:S(2)}, u32[]{:S(2)}) collective-permute-start(bf16[64,1024]{1,0:T(8,128)(2,1)S(1)} %get-tuple-element.305), channel_id=1, source_target_pairs={{0,4},{4,8},{8,12},{12,16},{16,20},{20,24},{24,28},{28,32},{32,36}... | collective-permute-start | bytes 393224 | tf_op jit(solution)/shard_map/ppermute | solution.py:168
  25.2 435.1 %reduce-scatter.5.cloned.1.call-start = ((), (), s32[]{:S(2)}) async-start(), calls=%async_computation.5 | async-start | bytes 9191424 | tf_op jit(solution)/shard_map/reduce_scatter | solution.py:416
  28.2 17.8 %collective-permute-start.2 = (bf16[656,512]{1,0:T(8,128)(2,1)S(1)}, bf16[656,512]{1,0:T(8,128)(2,1)S(1)}, u32[]{:S(2)}, u32[]{:S(2)}) collective-permute-start(bf16[656,512]{1,0:T(8,128)(2,1)S(1)} %get-tuple-element.178), channel_id=1, source_target_pairs={{1,0},{2,1},{3,2},{0,3},{5,4},{6,5},{7,6},{4,7},{9,8},{10,9},{11,1... | collective-permute-start | bytes 2015240 | tf_op jit(solution)/shard_map/ppermute | solution.py:649
  32.0 18.2 %collective-permute-start.3 = (bf16[656,512]{1,0:T(8,128)(2,1)S(1)}, bf16[656,512]{1,0:T(8,128)(2,1)S(1)}, u32[]{:S(2)}, u32[]{:S(2)}) collective-permute-start(bf16[656,512]{1,0:T(8,128)(2,1)S(1)} %get-tuple-element.178), channel_id=1, source_target_pairs={{0,1},{1,2},{2,3},{3,0},{4,5},{5,6},{6,7},{7,4},{8,9},{9,10},{10,1... | collective-permute-start | bytes 2015240 | tf_op jit(solution)/shard_map/ppermute | solution.py:649
  46.9 12.5 %collective-permute-start.5 = (bf16[656,256]{1,0:T(8,128)(2,1)}, bf16[656,256]{1,0:T(8,128)(2,1)}, u32[]{:S(2)}, u32[]{:S(2)}) collective-permute-start(bf16[656,256]{1,0:T(8,128)(2,1)} %slice.535), channel_id=1, source_target_pairs={{1,0},{2,1},{3,2},{0,3},{5,4},{6,5},{7,6},{4,7},{9,8},{10,9},{11,1... | collective-permute-start | bytes 1007624 | tf_op jit(solution)/shard_map/ppermute | solution.py:655
  51.9 13.6 %collective-permute-start.4 = (bf16[656,256]{1,0:T(8,128)(2,1)}, bf16[656,256]{1,0:T(8,128)(2,1)}, u32[]{:S(2)}, u32[]{:S(2)}) collective-permute-start(bf16[656,256]{1,0:T(8,128)(2,1)} %slice.534), channel_id=1, source_target_pairs={{0,1},{1,2},{2,3},{3,0},{4,5},{5,6},{6,7},{7,4},{8,9},{9,10},{10,1... | collective-permute-start | bytes 1007624 | tf_op jit(solution)/shard_map/ppermute | solution.py:654
  66.7 6.8 %collective-permute-start.6 = (bf16[2688,512]{1,0:T(8,128)(2,1)S(1)}, bf16[2688,512]{1,0:T(8,128)(2,1)}, u32[]{:S(2)}, u32[]{:S(2)}) collective-permute-start(bf16[2688,512]{1,0:T(8,128)(2,1)S(1)} %constant_dynamic-update-slice_fusion.19.down_own), channel_id=1, source_target_pairs={{0,64},{64,0},{1,65},{65,1},{2,66},{66,2},{3,67},{67,3},{4,68},{68... | collective-permute-start | bytes 8257544 | tf_op jit(solution)/shard_map/ppermute | solution.py:31
  100.8 15.7 %collective-permute-start.10 = (bf16[512,9472]{1,0:T(8,128)(2,1)}, bf16[512,9472]{1,0:T(8,128)(2,1)}, u32[]{:S(2)}, u32[]{:S(2)}) collective-permute-start(bf16[512,9472]{1,0:T(8,128)(2,1)} %all-gather.3.cloned.1.call-done.weight_own.gate_own.up_own), channel_id=1, source_target_pairs={{0,64},{64,0},{1,65},{65,1},{2,66},{66,2},{3,67},{67,3},{4,68},{68... | collective-permute-start | bytes 29097992 | tf_op jit(solution)/shard_map/ppermute | solution.py:31
  101.5 38.3 %collective-permute-start.11 = (bf16[656,512]{1,0:T(8,128)(2,1)}, bf16[656,512]{1,0:T(8,128)(2,1)}, u32[]{:S(2)}, u32[]{:S(2)}) collective-permute-start(bf16[656,512]{1,0:T(8,128)(2,1)} %get-tuple-element.82), channel_id=1, source_target_pairs={{0,1},{1,2},{2,3},{3,0},{4,5},{5,6},{6,7},{7,4},{8,9},{9,10},{10,1... | collective-permute-start | bytes 2015240 | tf_op jit(solution)/shard_map/ppermute | solution.py:649
  102.0 37.7 %collective-permute-start.12 = (bf16[656,512]{1,0:T(8,128)(2,1)}, bf16[656,512]{1,0:T(8,128)(2,1)}, u32[]{:S(2)}, u32[]{:S(2)}) collective-permute-start(bf16[656,512]{1,0:T(8,128)(2,1)} %get-tuple-element.82), channel_id=1, source_target_pairs={{1,0},{2,1},{3,2},{0,3},{5,4},{6,5},{7,6},{4,7},{9,8},{10,9},{11,1... | collective-permute-start | bytes 2015240 | tf_op jit(solution)/shard_map/ppermute | solution.py:649
  141.2 11.8 %collective-permute-start.14 = (bf16[656,256]{1,0:T(8,128)(2,1)S(1)}, bf16[656,256]{1,0:T(8,128)(2,1)S(1)}, u32[]{:S(2)}, u32[]{:S(2)}) collective-permute-start(bf16[656,256]{1,0:T(8,128)(2,1)S(1)} %slice.446), channel_id=1, source_target_pairs={{1,0},{2,1},{3,2},{0,3},{5,4},{6,5},{7,6},{4,7},{9,8},{10,9},{11,1... | collective-permute-start | bytes 1007624 | tf_op jit(solution)/shard_map/ppermute | solution.py:655
  144.2 11.9 %collective-permute-start.13 = (bf16[656,256]{1,0:T(8,128)(2,1)S(1)}, bf16[656,256]{1,0:T(8,128)(2,1)S(1)}, u32[]{:S(2)}, u32[]{:S(2)}) collective-permute-start(bf16[656,256]{1,0:T(8,128)(2,1)S(1)} %slice.445), channel_id=1, source_target_pairs={{0,1},{1,2},{2,3},{3,0},{4,5},{5,6},{6,7},{7,4},{8,9},{9,10},{10,1... | collective-permute-start | bytes 1007624 | tf_op jit(solution)/shard_map/ppermute | solution.py:654
  159.1 31.1 %collective-permute-start.15 = (bf16[2688,512]{1,0:T(8,128)(2,1)}, bf16[2688,512]{1,0:T(8,128)(2,1)}, u32[]{:S(2)}, u32[]{:S(2)}) collective-permute-start(bf16[2688,512]{1,0:T(8,128)(2,1)} %constant_dynamic-update-slice_fusion.16.down_own), channel_id=1, source_target_pairs={{0,64},{64,0},{1,65},{65,1},{2,66},{66,2},{3,67},{67,3},{4,68},{68... | collective-permute-start | bytes 8257544 | tf_op jit(solution)/shard_map/ppermute | solution.py:31
  161.6 10.1 %collective-permute-start.17 = (bf16[64,1024]{1,0:T(8,128)(2,1)S(1)}, bf16[64,1024]{1,0:T(8,128)(2,1)S(1)}, u32[]{:S(2)}, u32[]{:S(2)}) collective-permute-start(bf16[64,1024]{1,0:T(8,128)(2,1)S(1)} %get-tuple-element.286), channel_id=1, source_target_pairs={{4,0},{8,4},{12,8},{16,12},{20,16},{24,20},{28,24},{32,28},{36,32}... | collective-permute-start | bytes 393224 | tf_op jit(solution)/shard_map/ppermute | solution.py:172
  162.9 9.8 %collective-permute-start.16 = (bf16[64,1024]{1,0:T(8,128)(2,1)S(1)}, bf16[64,1024]{1,0:T(8,128)(2,1)S(1)}, u32[]{:S(2)}, u32[]{:S(2)}) collective-permute-start(bf16[64,1024]{1,0:T(8,128)(2,1)S(1)} %get-tuple-element.285), channel_id=1, source_target_pairs={{0,4},{4,8},{8,12},{12,16},{16,20},{20,24},{24,28},{28,32},{32,36}... | collective-permute-start | bytes 393224 | tf_op jit(solution)/shard_map/ppermute | solution.py:168
  192.3 7.5 %collective-permute-start.18 = (bf16[512,3072]{1,0:T(8,128)(2,1)S(1)}, bf16[512,3072]{1,0:T(8,128)(2,1)S(1)}, u32[]{:S(2)}, u32[]{:S(2)}) collective-permute-start(bf16[512,3072]{1,0:T(8,128)(2,1)S(1)} %slice.458), channel_id=1, source_target_pairs={{0,64},{64,0},{1,65},{65,1},{2,66},{66,2},{3,67},{67,3},{4,68},{68... | collective-permute-start | bytes 9437192 | tf_op jit(solution)/shard_map/ppermute | solution.py:31
  194.3 5.5 %collective-permute-start.19 = (bf16[512,1024]{1,0:T(8,128)(2,1)S(1)}, bf16[512,1024]{1,0:T(8,128)(2,1)S(1)}, u32[]{:S(2)}, u32[]{:S(2)}) collective-permute-start(bf16[512,1024]{1,0:T(8,128)(2,1)S(1)} %slice.459), channel_id=1, source_target_pairs={{0,64},{64,0},{1,65},{65,1},{2,66},{66,2},{3,67},{67,3},{4,68},{68... | collective-permute-start | bytes 3145736 | tf_op jit(solution)/shard_map/ppermute | solution.py:31
  199.8 15.3 %collective-permute-start.20 = (bf16[512,9472]{1,0:T(8,128)(2,1)}, bf16[512,9472]{1,0:T(8,128)(2,1)S(1)}, u32[]{:S(2)}, u32[]{:S(2)}) collective-permute-start(bf16[512,9472]{1,0:T(8,128)(2,1)} %all-gather.5.cloned.1.call-done.weight_own.gate_own.up_own), channel_id=1, source_target_pairs={{0,64},{64,0},{1,65},{65,1},{2,66},{66,2},{3,67},{67,3},{4,68},{68... | collective-permute-start | bytes 29097992 | tf_op jit(solution)/shard_map/ppermute | solution.py:31
  238.4 4.5 collective-permute-start.23
  250.1 213.5 %reduce-scatter.3.cloned.1.call-start = ((), (), s32[]{:S(2)}) async-start(), calls=%async_computation.4 | async-start | bytes 13647872 | tf_op jit(solution)/shard_map/reduce_scatter | solution.py:416
  262.5 15.4 %collective-permute-start.26 = (bf16[64,2048]{1,0:T(8,128)(2,1)S(1)}, bf16[64,2048]{1,0:T(8,128)(2,1)S(1)}, u32[]{:S(2)}, u32[]{:S(2)}) collective-permute-start(bf16[64,2048]{1,0:T(8,128)(2,1)S(1)} %get-tuple-element.110), channel_id=1, source_target_pairs={{4,0},{8,4},{12,8},{16,12},{20,16},{24,20},{28,24},{32,28},{36,32}... | collective-permute-start | bytes 786440 | tf_op jit(solution)/shard_map/ppermute | solution.py:172
  263.8 14.1 %collective-permute-start.25 = (bf16[64,2048]{1,0:T(8,128)(2,1)S(1)}, bf16[64,2048]{1,0:T(8,128)(2,1)S(1)}, u32[]{:S(2)}, u32[]{:S(2)}) collective-permute-start(bf16[64,2048]{1,0:T(8,128)(2,1)S(1)} %get-tuple-element.109), channel_id=1, source_target_pairs={{0,4},{4,8},{8,12},{12,16},{16,20},{20,24},{24,28},{28,32},{32,36}... | collective-permute-start | bytes 786440 | tf_op jit(solution)/shard_map/ppermute | solution.py:168
  268.0 38.2 %collective-permute-start.29 = (bf16[3,128,1024]{2,1,0:T(8,128)(2,1)S(1)}, bf16[3,128,1024]{2,1,0:T(8,128)(2,1)S(1)}, u32[]{:S(2)}, u32[]{:S(2)}) collective-permute-start(bf16[3,128,1024]{2,1,0:T(8,128)(2,1)S(1)} %pad_maximum_fusion.7.refs_2_.refs_0_), channel_id=1, source_target_pairs={{0,64},{64,0},{1,65},{65,1},{2,66},{66,2},{3,67},{67,3},{4,68},{68... | collective-permute-start | bytes 2359304 | tf_op jit(solution)/shard_map/ppermute | solution.py:31
  269.0 37.2 %collective-permute-start.30 = (bf16[128,2688]{1,0:T(8,128)(2,1)S(1)}, bf16[128,2688]{1,0:T(8,128)(2,1)S(1)}, u32[]{:S(2)}, u32[]{:S(2)}) collective-permute-start(bf16[128,2688]{1,0:T(8,128)(2,1)S(1)} %copy-done.44), channel_id=1, source_target_pairs={{0,64},{64,0},{1,65},{65,1},{2,66},{66,2},{3,67},{67,3},{4,68},{68... | collective-permute-start | bytes 2064392 | tf_op jit(solution)/shard_map/ppermute | solution.py:31
  297.6 10.0 %collective-permute-start.27 = (bf16[128,3200]{1,0:T(8,128)(2,1)S(1)}, bf16[128,3200]{1,0:T(8,128)(2,1)S(1)}, u32[]{:S(2)}, u32[]{:S(2)}) collective-permute-start(bf16[128,3200]{1,0:T(8,128)(2,1)S(1)} %get-tuple-element.190), channel_id=1, source_target_pairs={{0,64},{64,0},{1,65},{65,1},{2,66},{66,2},{3,67},{67,3},{4,68},{68... | collective-permute-start | bytes 2457608 | tf_op jit(solution)/shard_map/ppermute | solution.py:31
  313.5 10.3 %collective-permute-start.32 = (bf16[64,2048]{1,0:T(8,128)(2,1)S(1)}, bf16[64,2048]{1,0:T(8,128)(2,1)S(1)}, u32[]{:S(2)}, u32[]{:S(2)}) collective-permute-start(bf16[64,2048]{1,0:T(8,128)(2,1)S(1)} %get-tuple-element.124), channel_id=1, source_target_pairs={{4,0},{8,4},{12,8},{16,12},{20,16},{24,20},{28,24},{32,28},{36,32}... | collective-permute-start | bytes 786440 | tf_op jit(solution)/shard_map/ppermute | solution.py:172
  314.8 11.6 %collective-permute-start.31 = (bf16[64,2048]{1,0:T(8,128)(2,1)S(1)}, bf16[64,2048]{1,0:T(8,128)(2,1)S(1)}, u32[]{:S(2)}, u32[]{:S(2)}) collective-permute-start(bf16[64,2048]{1,0:T(8,128)(2,1)S(1)} %get-tuple-element.123), channel_id=1, source_target_pairs={{0,4},{4,8},{8,12},{12,16},{16,20},{20,24},{24,28},{28,32},{32,36}... | collective-permute-start | bytes 786440 | tf_op jit(solution)/shard_map/ppermute | solution.py:168
  326.9 8.8 %collective-permute-start.33 = (bf16[128,2048]{1,0:T(8,128)(2,1)S(1)}, bf16[128,2048]{1,0:T(8,128)(2,1)S(1)}, u32[]{:S(2)}, u32[]{:S(2)}) collective-permute-start(bf16[128,2048]{1,0:T(8,128)(2,1)S(1)} %get-tuple-element.204), channel_id=1, source_target_pairs={{0,64},{64,0},{1,65},{65,1},{2,66},{66,2},{3,67},{67,3},{4,68},{68... | collective-permute-start | bytes 1572872 | tf_op jit(solution)/shard_map/ppermute | solution.py:31
  362.5 26.4 %collective-permute-start.40 = (bf16[16,16,2176]{2,1,0:T(8,128)(2,1)}, bf16[16,16,2176]{2,1,0:T(8,128)(2,1)}, u32[]{:S(2)}, u32[]{:S(2)}) collective-permute-start(bf16[16,16,2176]{2,1,0:T(8,128)(2,1)} %get-tuple-element.184), channel_id=1, source_target_pairs={{0,3},{1,0},{2,1},{3,2},{4,7},{5,4},{6,5},{7,6},{8,11},{9,8},{10,9... | collective-permute-start | bytes 3342344 | tf_op jit(solution)/shard_map/ppermute | solution.py:577
  365.2 26.6 %collective-permute-start.39 = (bf16[16,16,2176]{2,1,0:T(8,128)(2,1)}, bf16[16,16,2176]{2,1,0:T(8,128)(2,1)}, u32[]{:S(2)}, u32[]{:S(2)}) collective-permute-start(bf16[16,16,2176]{2,1,0:T(8,128)(2,1)} %get-tuple-element.185), channel_id=1, source_target_pairs={{0,2},{1,3},{2,0},{3,1},{4,6},{5,7},{6,4},{7,5},{8,10},{9,11},{10,... | collective-permute-start | bytes 3342344 | tf_op jit(solution)/shard_map/ppermute | solution.py:577
  365.8 51.8 %collective-permute-start.38 = (bf16[16,16,2176]{2,1,0:T(8,128)(2,1)}, bf16[16,16,2176]{2,1,0:T(8,128)(2,1)}, u32[]{:S(2)}, u32[]{:S(2)}) collective-permute-start(bf16[16,16,2176]{2,1,0:T(8,128)(2,1)} %get-tuple-element.183), channel_id=1, source_target_pairs={{0,1},{1,2},{2,3},{3,0},{4,5},{5,6},{6,7},{7,4},{8,9},{9,10},{10,1... | collective-permute-start | bytes 3342344 | tf_op jit(solution)/shard_map/ppermute | solution.py:577
  420.5 24.5 %collective-permute-start.43 = (bf16[4,16,2176]{2,1,0:T(8,128)(2,1)S(1)}, bf16[4,16,2176]{2,1,0:T(8,128)(2,1)S(1)}, u32[]{:S(2)}, u32[]{:S(2)}) collective-permute-start(bf16[4,16,2176]{2,1,0:T(8,128)(2,1)S(1)} %get-tuple-element.200), channel_id=1, source_target_pairs={{0,12},{4,0},{8,4},{12,8},{16,28},{20,16},{24,20},{28,24},{32,44},... | collective-permute-start | bytes 835592 | tf_op jit(solution)/shard_map/ppermute | solution.py:577
  428.8 16.2 %collective-permute-start.42 = (bf16[4,16,2176]{2,1,0:T(8,128)(2,1)S(1)}, bf16[4,16,2176]{2,1,0:T(8,128)(2,1)S(1)}, u32[]{:S(2)}, u32[]{:S(2)}) collective-permute-start(bf16[4,16,2176]{2,1,0:T(8,128)(2,1)S(1)} %get-tuple-element.201), channel_id=1, source_target_pairs={{0,8},{4,12},{8,0},{12,4},{16,24},{20,28},{24,16},{28,20},{32,40},... | collective-permute-start | bytes 835592 | tf_op jit(solution)/shard_map/ppermute | solution.py:577
  428.8 20.9 %collective-permute-start.41 = (bf16[4,16,2176]{2,1,0:T(8,128)(2,1)S(1)}, bf16[4,16,2176]{2,1,0:T(8,128)(2,1)S(1)}, u32[]{:S(2)}, u32[]{:S(2)}) collective-permute-start(bf16[4,16,2176]{2,1,0:T(8,128)(2,1)S(1)} %get-tuple-element.199), channel_id=1, source_target_pairs={{0,4},{4,8},{8,12},{12,0},{16,20},{20,24},{24,28},{28,16},{32,36},... | collective-permute-start | bytes 835592 | tf_op jit(solution)/shard_map/ppermute | solution.py:577
  449.9 7.5 %collective-permute-start.46 = (bf16[16,2176]{1,0:T(8,128)(2,1)S(1)}, bf16[16,2176]{1,0:T(8,128)(2,1)S(1)}, u32[]{:S(2)}, u32[]{:S(2)}) collective-permute-start(bf16[16,2176]{1,0:T(8,128)(2,1)S(1)} %get-tuple-element.249), channel_id=1, source_target_pairs={{0,48},{4,52},{8,56},{12,60},{16,0},{20,4},{24,8},{28,12},{32,16},... | collective-permute-start | bytes 208904 | tf_op jit(solution)/shard_map/ppermute | solution.py:577
  454.4 4.7 collective-permute-start.45
  455.0 5.1 %collective-permute-start.44 = (bf16[16,2176]{1,0:T(8,128)(2,1)S(1)}, bf16[16,2176]{1,0:T(8,128)(2,1)S(1)}, u32[]{:S(2)}, u32[]{:S(2)}) collective-permute-start(bf16[16,2176]{1,0:T(8,128)(2,1)S(1)} %get-tuple-element.248), channel_id=1, source_target_pairs={{0,16},{4,20},{8,24},{12,28},{16,32},{20,36},{24,40},{28,44},{32,4... | collective-permute-start | bytes 208904 | tf_op jit(solution)/shard_map/ppermute | solution.py:577
  455.9 26.8 %collective-permute-start.34 = (f32[128,1024]{1,0:T(8,128)S(1)}, f32[128,1024]{1,0:T(8,128)S(1)}, u32[]{:S(2)}, u32[]{:S(2)}) collective-permute-start(f32[128,1024]{1,0:T(8,128)S(1)} %get-tuple-element.167), channel_id=1, source_target_pairs={{0,64},{64,0},{1,65},{65,1},{2,66},{66,2},{3,67},{67,3},{4,68},{68... | collective-permute-start | bytes 1572872 | tf_op jit(solution)/shard_map/ppermute | solution.py:31
  462.1 5.1 %collective-permute-start.49 = (bf16[16,4224]{1,0:T(8,128)(2,1)}, bf16[16,4224]{1,0:T(8,128)(2,1)S(1)}, u32[]{:S(2)}, u32[]{:S(2)}) collective-permute-start(bf16[16,4224]{1,0:T(8,128)(2,1)} %get-tuple-element.210), channel_id=1, source_target_pairs={{0,3},{1,0},{2,1},{3,2},{4,7},{5,4},{6,5},{7,6},{8,11},{9,8},{10,9... | collective-permute-start | bytes 405512 | tf_op jit(solution)/shard_map/ppermute | solution.py:560
  462.1 6.4 %collective-permute-start.48 = (bf16[16,4224]{1,0:T(8,128)(2,1)}, bf16[16,4224]{1,0:T(8,128)(2,1)S(1)}, u32[]{:S(2)}, u32[]{:S(2)}) collective-permute-start(bf16[16,4224]{1,0:T(8,128)(2,1)} %get-tuple-element.211), channel_id=1, source_target_pairs={{0,2},{1,3},{2,0},{3,1},{4,6},{5,7},{6,4},{7,5},{8,10},{9,11},{10,... | collective-permute-start | bytes 405512 | tf_op jit(solution)/shard_map/ppermute | solution.py:560
  462.3 7.8 %collective-permute-start.47 = (bf16[16,4224]{1,0:T(8,128)(2,1)S(1)}, bf16[16,4224]{1,0:T(8,128)(2,1)}, u32[]{:S(2)}, u32[]{:S(2)}) collective-permute-start(bf16[16,4224]{1,0:T(8,128)(2,1)S(1)} %get-tuple-element.209), channel_id=1, source_target_pairs={{0,1},{1,2},{2,3},{3,0},{4,5},{5,6},{6,7},{7,4},{8,9},{9,10},{10,1... | collective-permute-start | bytes 405512 | tf_op jit(solution)/shard_map/ppermute | solution.py:560
  464.7 8.1 %collective-permute-start.37 = (bf16[16,6272]{1,0:T(8,128)(2,1)S(1)}, bf16[16,6272]{1,0:T(8,128)(2,1)S(1)}, u32[]{:S(2)}, u32[]{:S(2)}) collective-permute-start(bf16[16,6272]{1,0:T(8,128)(2,1)S(1)} %get-tuple-element.207), channel_id=1, source_target_pairs={{0,3},{1,0},{2,1},{3,2},{4,7},{5,4},{6,5},{7,6},{8,11},{9,8},{10,9... | collective-permute-start | bytes 602120 | tf_op jit(solution)/shard_map/ppermute | solution.py:560
  467.2 7.5 %collective-permute-start.36 = (bf16[16,6272]{1,0:T(8,128)(2,1)S(1)}, bf16[16,6272]{1,0:T(8,128)(2,1)S(1)}, u32[]{:S(2)}, u32[]{:S(2)}) collective-permute-start(bf16[16,6272]{1,0:T(8,128)(2,1)S(1)} %get-tuple-element.208), channel_id=1, source_target_pairs={{0,2},{1,3},{2,0},{3,1},{4,6},{5,7},{6,4},{7,5},{8,10},{9,11},{10,... | collective-permute-start | bytes 602120 | tf_op jit(solution)/shard_map/ppermute | solution.py:560
  468.5 10.7 %collective-permute-start.35 = (bf16[16,6272]{1,0:T(8,128)(2,1)S(1)}, bf16[16,6272]{1,0:T(8,128)(2,1)S(1)}, u32[]{:S(2)}, u32[]{:S(2)}) collective-permute-start(bf16[16,6272]{1,0:T(8,128)(2,1)S(1)} %get-tuple-element.206), channel_id=1, source_target_pairs={{0,1},{1,2},{2,3},{3,0},{4,5},{5,6},{6,7},{7,4},{8,9},{9,10},{10,1... | collective-permute-start | bytes 602120 | tf_op jit(solution)/shard_map/ppermute | solution.py:560
  (84 other events, 673.3 us)
Sparse Core Ops, SparseCore 0:
  13.5 87.3 all-gather.2
  104.2 85.9 all-gather.4
  250.2 90.8 reduce-scatter.4
  344.8 108.6 reduce-scatter.2
where the time goes:
time: 505 us; the launch traced here: 495 us
  waiting for transfers between devices  211 us (42%)
  Pallas kernels  86.4 us (17%)
  starting transfers between devices  81.3 us (16%)
  local copies, waits for them, and re-layouts  59.9 us (12%)
  other arithmetic  29.6 us (6%)
  between operations  15.9 us (3%)
  matrix products  11 us (2%)
    ppermute x9, waiting for transfers between devices, phase(): lax.ppermute(part(step), axis, route(step)).astype(jnp.float32)  69.1 us
    pallas_call x12, Pallas kernels, grid_call(): pl.pallas_call(kernel, grid_spec=pltpu.PrefetchScalarGridSpec(num_scalar_...  68.9 us
    all_gather x2, waiting for transfers between devices, gathered(): return lax.all_gather(piece, ('wshard', 'seq'), axis=0, tiled=True)  44.7 us
    unnamed x169, local copies, waits for them, and re-layouts  32.2 us
    ppermute x20, waiting for transfers between devices, swapped(): return lax.ppermute(array, 'section', SWAP)  32.1 us
    ppermute x20, starting transfers between devices, swapped(): return lax.ppermute(array, 'section', SWAP)  21.4 us
    ppermute x4, waiting for transfers between devices, to_previous(): return lax.ppermute(array, 'seq', [(i + 1, i) for i in range(SEQ_DEV - 1)])  19.3 us
    ppermute x9, starting transfers between devices, phase(): lax.ppermute(part(step), axis, route(step)).astype(jnp.float32)  18.6 us
  transfers between devices with their start and end apart: 55, of which 34 were waited for; matrix products, arithmetic and copies ran while one was open for 12% of the time, Pallas kernels for 13%

commit v1 on v0

--- a/solution.py
+++ b/solution.py
@@ -131,7 +131,7 @@
             after[:, columns] = piece[HALO + rows :].astype(jnp.bfloat16)
 
 
-params = pltpu.CompilerParams(vmem_limit_bytes=40 * 1024 * 1024)
+params = pltpu.CompilerParams(vmem_limit_bytes=48 * 1024 * 1024)
 
 
 def attend(query_seg, key_seg, qkv):
@@ -420,7 +420,7 @@
 ROW_GROUPS = PAD_ROWS // 16
 
 
-def weight_grads(name, items, grads, total, product=None, gains=None, base=None):
+def weight_grads(name, items, grads, total, product=None, base=None):
     count, width = items[0][0].shape[1:]
     block = 256
     in_specs, args = ([], [])
@@ -440,9 +440,6 @@
             pltpu.VMEM((FF_PAD, half), jnp.float32),
             pltpu.VMEM((width, ROW_GROUPS * half), jnp.bfloat16),
         ]
-    if gains is not None:
-        in_specs.append(rows_at(block, gains[0].shape[1]))
-        args.append(gains[0])
     aliases = {}
     columns = total
     if base is not None:
@@ -489,9 +486,6 @@
             out[:, place : place + ROW_GROUPS * half] = rows[-1][
                 pl.ds(pl.multiple_of(step * block, block), block)
             ]
-        if gains is not None:
-            place = gains[1]
-            out[:, place : place + gains[0].shape[1]] = rest[2 if product is not None else 0][...]
 
     return grid_call(
         kernel,
@@ -758,7 +752,7 @@
         )
         side_grads.append(
             functools.partial(
-                weight_grads, "side_grads", [out_item[:-1] + (0,)], pairs, side_at + 128, product
+                weight_grads, "side_grads", [out_item[:-1] + (0,)], pairs, side_at, product
             )
         )
         return (hidden_pair[1], attn_pair1[1], *kept0[-1])
@@ -768,7 +762,8 @@
         late_grads.extend(
             weight_grads("attn_grads", attn_items(kept0, 0, 0), [attn_pair], total, base=base)
         )
-        return late_grads[1:]
+        side_grads.extend(side_grads.pop()())
+        return (late_grads[1], side_grads[1])
 
     grads0, _, _, gains0 = layer_backward(
         grads1, kept0, gain_pairs[0], weights[0], segs, on_first, first, make_joint, make_late
@@ -776,8 +771,8 @@
     late = seq_sum(late_grads[0])
     gains = jnp.concatenate([gains0, gains1], axis=0)
     gains = jnp.pad(gains, ((0, 128 - gains.shape[0]), (0, 0))).T.astype(jnp.bfloat16)
-    side = side_grads[0](gains=(gains, side_at))[0]
-    side_total = summed_by_steps(side, seq_place, w_place)
+    side_total = summed_by_steps(side_grads[0], seq_place, w_place)
+    gain_part = summed_by_steps(gains, seq_place, w_place)
 
     def placed(first, second):
         mine, give = (by_core(first, second), by_core(second, first))
@@ -788,11 +783,10 @@
     section_input_grads = placed(grads0, grads1)
 
     early_total, late_total = (summed_over_w(early, w_place), summed_over_w(late, w_place))
-    gain_part = side_total[:, side_at:]
     of_first = jnp.concatenate(
         [
             late_total[:, :second_at], gain_part, late_total[:, hidden_at:],
-            side_total[:, out_cols:side_at],
+            side_total[:, out_cols:],
         ],
         axis=1,
     )

time: 505 us -> 502 us (level)
  the two profiles are of different devices: /device:TPU:1 before, /device:TPU:3 now
where the time goes in v1:
time: 502 us; the launch traced here: 492 us
  waiting for transfers between devices  203 us (40%)
  starting transfers between devices  96.5 us (19%)
  Pallas kernels  95.1 us (19%)
  local copies, waits for them, and re-layouts  39 us (8%)
  other arithmetic  31.6 us (6%)
  between operations  15.7 us (3%)
  matrix products  11 us (2%)
    pallas_call x12, Pallas kernels, grid_call(): pl.pallas_call(kernel, grid_spec=pltpu.PrefetchScalarGridSpec(num_scalar_...  76 us
    ppermute x18, waiting for transfers between devices, phase(): lax.ppermute(part(step), axis, route(step)).astype(jnp.float32)  55.8 us
    all_gather x2, waiting for transfers between devices, gathered(): return lax.all_gather(piece, ('wshard', 'seq'), axis=0, tiled=True)  45.7 us
    ppermute x18, starting transfers between devices, phase(): lax.ppermute(part(step), axis, route(step)).astype(jnp.float32)  34.5 us
    ppermute x20, waiting for transfers between devices, swapped(): return lax.ppermute(array, 'section', SWAP)  32 us
    ppermute x20, starting transfers between devices, swapped(): return lax.ppermute(array, 'section', SWAP)  20 us
    ppermute x4, waiting for transfers between devices, to_previous(): return lax.ppermute(array, 'seq', [(i + 1, i) for i in range(SEQ_DEV - 1)])  18.6 us
    ppermute x2, waiting for transfers between devices, neighbours(): lax.ppermute(piece, 'wshard', w_down)  13.8 us
  transfers between devices with their start and end apart: 64, of which 34 were waited for; matrix products, arithmetic and copies ran while one was open for 13% of the time, Pallas kernels for 15%

profile of v1, /device:TPU:3, one launch (start us, length us, event | category | flops | bytes accessed | tf_op | source)
XLA Modules:
  0.0 491.7 jit_solution(3072552851972646488)
XLA Ops:
  17.4 3.2 collective-permute-start.8
  27.5 3.8 collective-permute-start.2
  31.4 13.8 %collective-permute-done.2 = bf16[656,512]{1,0:T(8,128)(2,1)S(1)} collective-permute-done((bf16[656,512]{1,0:T(8,128)(2,1)S(1)}, bf16[656,512]{1,0:T(8,128)(2,1)S(1)}, u32[]{:S(2)}, u32[]{:S(2)}) %collective-permute-start.2) | collective-permute-done | bytes 671776 | tf_op jit(solution)/shard_map/ppermute | solution.py:643
  46.0 3.4 collective-permute-start.5
  52.2 6.4 %collective-permute-done.5 = bf16[656,256]{1,0:T(8,128)(2,1)} collective-permute-done((bf16[656,256]{1,0:T(8,128)(2,1)}, bf16[656,256]{1,0:T(8,128)(2,1)}, u32[]{:S(2)}, u32[]{:S(2)}) %collective-permute-start.5) | collective-permute-done | bytes 335904 | tf_op jit(solution)/shard_map/ppermute | solution.py:649
  58.6 6.3 %collective-permute-done.4 = bf16[656,256]{1,0:T(8,128)(2,1)} collective-permute-done((bf16[656,256]{1,0:T(8,128)(2,1)}, bf16[656,256]{1,0:T(8,128)(2,1)}, u32[]{:S(2)}, u32[]{:S(2)}) %collective-permute-start.4) | collective-permute-done | bytes 335904 | tf_op jit(solution)/shard_map/ppermute | solution.py:648
  68.0 4.7 collective-permute-done.6.down_other
  72.7 27.5 %all-gather.3.cloned.1.call-done.weight_own.gate_own.up_own = bf16[512,9472]{1,0:T(8,128)(2,1)} async-done(((bf16[8,9472]{1,0:T(8,128)(2,1)}), bf16[512,9472]{1,0:T(8,128)(2,1)}) %all-gather.3.cloned.1.call-update) | async-done | bytes 9699344 | tf_op jit(solution)/shard_map/all_gather | solution.py:632
  105.0 10.9 %collective-permute-done.10.weight_other.gate_other.up_other = bf16[512,9472]{1,0:T(8,128)(2,1)} collective-permute-done((bf16[512,9472]{1,0:T(8,128)(2,1)}, bf16[512,9472]{1,0:T(8,128)(2,1)}, u32[]{:S(2)}, u32[]{:S(2)}) %collective-permute-start.10) | collective-permute-done | bytes 9699360 | tf_op jit(solution)/shard_map/ppermute | solution.py:31
  115.9 4.7 qkv.2
  120.6 2.9 attend.2
  127.4 8.1 %hidden.2 = (f32[128,2688]{1,0:T(8,128)S(1)}, f32[128,2688]{1,0:T(8,128)S(1)}, bf16[128,2688]{1,0:T(8,128)(2,1)S(1)}, f32[128,1024]{1,0:T(8,128)S(1)}) custom-call(s32[1]{0:T(128)} %bitcast.first, bf16[128,512]{1,0:T(8,128)(2,1)S(1)} %get-tuple-element.293.own, bf16[128,512]{1,0:T(8,128)(2,1)S(1)} %get-tuple-element.292.other, ...), custom_call_target="tpu_custom_call" | custom-call | tf_op jit(solution)/shard_map/hidden/pallas_call | solution.py:181
  145.2 5.5 %collective-permute-done.14 = bf16[656,256]{1,0:T(8,128)(2,1)S(1)} collective-permute-done((bf16[656,256]{1,0:T(8,128)(2,1)S(1)}, bf16[656,256]{1,0:T(8,128)(2,1)S(1)}, u32[]{:S(2)}, u32[]{:S(2)}) %collective-permute-start.14) | collective-permute-done | bytes 335904 | tf_op jit(solution)/shard_map/ppermute | solution.py:649
  150.7 3.0 collective-permute-done.13
  161.0 3.1 collective-permute-start.16
  164.1 4.8 collective-permute-done.17
  171.1 18.2 %all-gather.5.cloned.1.call-done.weight_own.gate_own.up_own = bf16[512,9472]{1,0:T(8,128)(2,1)} async-done(((bf16[8,9472]{1,0:T(8,128)(2,1)}), bf16[512,9472]{1,0:T(8,128)(2,1)}) %all-gather.5.cloned.1.call-update) | async-done | bytes 9699344 | tf_op jit(solution)/shard_map/all_gather | solution.py:632
  193.6 5.4 %collective-permute-done.19 = bf16[512,1024]{1,0:T(8,128)(2,1)S(1)} collective-permute-done((bf16[512,1024]{1,0:T(8,128)(2,1)S(1)}, bf16[512,1024]{1,0:T(8,128)(2,1)S(1)}, u32[]{:S(2)}, u32[]{:S(2)}) %collective-permute-start.19) | collective-permute-done | bytes 1048608 | tf_op jit(solution)/shard_map/ppermute | solution.py:31
  199.8 4.8 qkv.3
  204.7 2.9 attend.3
  211.0 3.4 collective-permute-done.20.gate_other.up_other
  214.5 8.0 %hidden.3 = (f32[128,2688]{1,0:T(8,128)S(1)}, f32[128,2688]{1,0:T(8,128)S(1)}, bf16[128,2688]{1,0:T(8,128)(2,1)S(1)}, f32[128,1024]{1,0:T(8,128)S(1)}) custom-call(s32[1]{0:T(128)} %bitcast.first, bf16[128,512]{1,0:T(8,128)(2,1)S(1)} %get-tuple-element.273.own, bf16[128,512]{1,0:T(8,128)(2,1)S(1)} %get-tuple-element.272.other, ...), custom_call_target="tpu_custom_call" | custom-call | tf_op jit(solution)/shard_map/hidden/pallas_call | solution.py:181
  223.3 9.6 %hidden_back.2 = (bf16[128,2688]{1,0:T(8,128)(2,1)S(1)}, bf16[128,2688]{1,0:T(8,128)(2,1)S(1)}, f32[128,1024]{1,0:T(8,128)S(1)}) custom-call(s32[1]{0:T(128)} %bitcast.first, bf16[128,512]{1,0:T(8,128)(2,1)S(1)} %get-tuple-element.267.grad_own, bf16[128,512]{1,0:T(8,128)(2,1)S(1)} %get-tuple-element.268.grad_other, ...), custom_call_target="tpu_custom_call" | custom-call | tf_op jit(solution)/shard_map/hidden_back/pallas_call | solution.py:181
  237.7 5.9 %hidden_grads.1 = (bf16[1024,4224]{1,0:T(8,128)(2,1)}, f32[8,128]{1,0:T(8,128)S(1)}) custom-call(bf16[3,128,1024]{2,1,0:T(8,128)(2,1)S(1)} %pad_maximum_fusion.6.refs_0_, bf16[3,128,1024]{2,1,0:T(8,128)(2,1)S(1)} %collective-permute-done.22.refs_1_, bf16[128,3200]{1,0:T(8,128)(2,1)S(1)} %get-tuple-element.194.refs_2_, ...), custom_call_target="tpu_custom_call" | custom-call | tf_op jit(solution)/shard_map/hidden_grads/pallas_call | solution.py:181
  250.3 5.8 %attend_back.2 = (bf16[128,1024]{1,0:T(8,128)(2,1)S(1)}, f32[128,2048]{1,0:T(8,128)S(1)}, bf16[64,2048]{1,0:T(8,128)(2,1)S(1)}, bf16[64,2048]{1,0:T(8,128)(2,1)S(1)}) custom-call(s32[128,1]{1,0:T(8,128)S(1)} %copy.35.query_seg, s32[1,256]{1,0:T(1,128)S(1)} %bitcast.162, bf16[256,3072]{1,0:T(8,128)(2,1)S(1)} %qkv.3, f32[128,1024]{1,0:T(8,128)S(1)} %copy-done.27, ...), custom_call_target="tpu_custom_call" | custom-call | tf_op jit(solution)/shard_map/attend_back/pallas_call | solution.py:152
  256.1 3.4 collective-permute-start.26
  262.7 8.2 %collective-permute-done.26 = bf16[64,2048]{1,0:T(8,128)(2,1)S(1)} collective-permute-done((bf16[64,2048]{1,0:T(8,128)(2,1)S(1)}, bf16[64,2048]{1,0:T(8,128)(2,1)S(1)}, u32[]{:S(2)}, u32[]{:S(2)}) %collective-permute-start.26) | collective-permute-done | bytes 262176 | tf_op jit(solution)/shard_map/ppermute | solution.py:172
  272.8 5.1 %qkv_back.2 = f32[128,1024]{1,0:T(8,128)S(1)} custom-call(s32[1]{0:T(128)} %bitcast.first, bf16[128,3072]{1,0:T(8,128)(2,1)S(1)} %pad_maximum_fusion.grad, bf16[512,9472]{1,0:T(8,128)(2,1)} %all-gather.5.cloned.1.call-done.weight_own.gate_own.up_own, bf16[512,3072]{1,0:T(8,128)(2,1)S(1)} %copy-done.2), custom_call_target="tpu_custom_call" | custom-call | tf_op jit(solution)/shard_map/qkv_back/pallas_call | solution.py:181
  279.8 10.1 %hidden_back.3 = (bf16[128,2688]{1,0:T(8,128)(2,1)S(1)}, bf16[128,2688]{1,0:T(8,128)(2,1)S(1)}, f32[128,1024]{1,0:T(8,128)S(1)}) custom-call(s32[1]{0:T(128)} %bitcast.first, bf16[128,512]{1,0:T(8,128)(2,1)S(1)} %get-tuple-element.261.grad_own, bf16[128,512]{1,0:T(8,128)(2,1)S(1)} %get-tuple-element.262.grad_other, f32[128,2688]{1,0:T(8,128)S(1)} %copy-done.18, ...), custom_call_target="tpu_custom_call" | custom-call | tf_op jit(solution)/shard_map/hidden_back/pallas_call | solution.py:181
  290.2 3.2 collective-permute-start.27
  301.1 7.4 %attend_back.3 = (bf16[128,1024]{1,0:T(8,128)(2,1)S(1)}, f32[128,2048]{1,0:T(8,128)S(1)}, bf16[64,2048]{1,0:T(8,128)(2,1)S(1)}, bf16[64,2048]{1,0:T(8,128)(2,1)S(1)}) custom-call(s32[128,1]{1,0:T(8,128)S(1)} %copy.35.query_seg, s32[1,256]{1,0:T(1,128)S(1)} %bitcast.163, bf16[256,3072]{1,0:T(8,128)(2,1)} %copy-done, f32[128,1024]{1,0:T(8,128)S(1)} %copy-done.29, ...), custom_call_target="tpu_custom_call" | custom-call | tf_op jit(solution)/shard_map/attend_back/pallas_call | solution.py:152
  310.5 3.4 collective-permute-start.31
  313.9 4.3 collective-permute-done.32
  324.0 6.3 %joint_grads.1 = (bf16[1024,6272]{1,0:T(8,128)(2,1)}, f32[8,128]{1,0:T(8,128)}) custom-call(bf16[3,128,1024]{2,1,0:T(8,128)(2,1)S(1)} %copy-done.4, bf16[3,128,1024]{2,1,0:T(8,128)(2,1)S(1)} %copy-done.6, bf16[3,128,1024]{2,1,0:T(8,128)(2,1)S(1)} %pad_maximum_fusion.7.refs_2_.refs_0_, ...), custom_call_target="tpu_custom_call" | custom-call | tf_op jit(solution)/shard_map/joint_grads/pallas_call | solution.py:181
  330.3 3.6 attn_grads.1
  342.5 4.2 side_grads.1
  346.6 3.8 dynamic-slice_bitcast_fusion.2
  354.2 5.6 %qkv_back.3 = f32[128,1024]{1,0:T(8,128)S(1)} custom-call(s32[1]{0:T(128)} %bitcast.first, bf16[128,3072]{1,0:T(8,128)(2,1)S(1)} %pad_maximum_fusion.1.grad, bf16[512,9472]{1,0:T(8,128)(2,1)} %all-gather.3.cloned.1.call-done.weight_own.gate_own.up_own, bf16[512,9472]{1,0:T(8,128)(2,1)} %collective-permute-done.10.weight_other.gate_other.up_other, ...), custom_call_target="tpu_custom_call" | custom-call | tf_op jit(solution)/shard_map/qkv_back/pallas_call | solution.py:181
  364.0 36.6 %collective-permute-done.40 = bf16[16,16,128]{2,1,0:T(8,128)(2,1)S(1)} collective-permute-done((bf16[16,16,128]{2,1,0:T(8,128)(2,1)S(1)}, bf16[16,16,128]{2,1,0:T(8,128)(2,1)S(1)}, u32[]{:S(2)}, u32[]{:S(2)}) %collective-permute-start.40) | collective-permute-done | bytes 65568 | tf_op jit(solution)/shard_map/ppermute | solution.py:571
  406.4 6.4 %collective-permute-start.42 = (bf16[4,16,128]{2,1,0:T(8,128)(2,1)S(1)}, bf16[4,16,128]{2,1,0:T(8,128)(2,1)S(1)}, u32[]{:S(2)}, u32[]{:S(2)}) collective-permute-start(bf16[4,16,128]{2,1,0:T(8,128)(2,1)S(1)} %get-tuple-element.318), channel_id=1, source_target_pairs={{0,8},{4,12},{8,0},{12,4},{16,24},{20,28},{24,16},{28,20},{32,40},... | collective-permute-start | bytes 49160 | tf_op jit(solution)/shard_map/ppermute | solution.py:571
  420.6 3.9 collective-permute-start.46
  424.4 5.7 %collective-permute-done.52 = bf16[4,16,2048]{2,1,0:T(8,128)(2,1)S(1)} collective-permute-done((bf16[4,16,2048]{2,1,0:T(8,128)(2,1)S(1)}, bf16[4,16,2048]{2,1,0:T(8,128)(2,1)S(1)}, u32[]{:S(2)}, u32[]{:S(2)}) %collective-permute-start.52) | collective-permute-done | bytes 262176 | tf_op jit(solution)/shard_map/ppermute | solution.py:571
  430.2 5.7 %collective-permute-start.45 = (bf16[16,128]{1,0:T(8,128)(2,1)S(1)}, bf16[16,128]{1,0:T(8,128)(2,1)S(1)}, u32[]{:S(2)}, u32[]{:S(2)}) collective-permute-start(bf16[16,128]{1,0:T(8,128)(2,1)S(1)} %get-tuple-element.321), channel_id=1, source_target_pairs={{0,32},{4,36},{8,40},{12,44},{16,48},{20,52},{24,56},{28,60},{32,0... | collective-permute-start | bytes 12296 | tf_op jit(solution)/shard_map/ppermute | solution.py:571
  435.9 5.6 %collective-permute-done.51 = bf16[4,16,2048]{2,1,0:T(8,128)(2,1)S(1)} collective-permute-done((bf16[4,16,2048]{2,1,0:T(8,128)(2,1)S(1)}, bf16[4,16,2048]{2,1,0:T(8,128)(2,1)S(1)}, u32[]{:S(2)}, u32[]{:S(2)}) %collective-permute-start.51) | collective-permute-done | bytes 262176 | tf_op jit(solution)/shard_map/ppermute | solution.py:571
  441.5 3.1 collective-permute-start.44
  464.7 3.7 collective-permute-done.37
  468.4 3.8 collective-permute-done.35
  473.4 4.4 collective-permute-start.59
  (383 shorter events, 152.2 us)
Async XLA Ops:
  7.2 93.0 %all-gather.3.cloned.1.call-start = ((), (), s32[]{:S(2)}) async-start(), calls=%async_computation.2 | async-start | bytes 9850880 | tf_op jit(solution)/shard_map/all_gather | solution.py:632
  12.6 176.7 %all-gather.5.cloned.1.call-start = ((), (), s32[]{:S(2)}) async-start(), calls=%async_computation.3 | async-start | bytes 9850880 | tf_op jit(solution)/shard_map/all_gather | solution.py:632
  13.2 11.4 %collective-permute-start.1 = (bf16[656,512]{1,0:T(8,128)(2,1)S(1)}, bf16[656,512]{1,0:T(8,128)(2,1)}, u32[]{:S(2)}, u32[]{:S(2)}) collective-permute-start(bf16[656,512]{1,0:T(8,128)(2,1)S(1)} %select_bitcast_fusion), channel_id=1, source_target_pairs={{0,64},{64,0},{1,65},{65,1},{2,66},{66,2},{3,67},{67,3},{4,68},{68... | collective-permute-start | bytes 2015240 | tf_op jit(solution)/shard_map/ppermute | solution.py:31
  15.3 6.6 %collective-permute-start.9 = (bf16[64,1024]{1,0:T(8,128)(2,1)S(1)}, bf16[64,1024]{1,0:T(8,128)(2,1)S(1)}, u32[]{:S(2)}, u32[]{:S(2)}) collective-permute-start(bf16[64,1024]{1,0:T(8,128)(2,1)S(1)} %get-tuple-element.311), channel_id=1, source_target_pairs={{4,0},{8,4},{12,8},{16,12},{20,16},{24,20},{28,24},{32,28},{36,32}... | collective-permute-start | bytes 393224 | tf_op jit(solution)/shard_map/ppermute | solution.py:172
  24.5 427.8 %reduce-scatter.5.cloned.1.call-start = ((), (), s32[]{:S(2)}) async-start(), calls=%async_computation.5 | async-start | bytes 9191424 | tf_op jit(solution)/shard_map/reduce_scatter | solution.py:416
  27.5 17.6 %collective-permute-start.2 = (bf16[656,512]{1,0:T(8,128)(2,1)S(1)}, bf16[656,512]{1,0:T(8,128)(2,1)S(1)}, u32[]{:S(2)}, u32[]{:S(2)}) collective-permute-start(bf16[656,512]{1,0:T(8,128)(2,1)S(1)} %get-tuple-element.180), channel_id=1, source_target_pairs={{1,0},{2,1},{3,2},{0,3},{5,4},{6,5},{7,6},{4,7},{9,8},{10,9},{11,1... | collective-permute-start | bytes 2015240 | tf_op jit(solution)/shard_map/ppermute | solution.py:643
  31.4 18.0 %collective-permute-start.3 = (bf16[656,512]{1,0:T(8,128)(2,1)S(1)}, bf16[656,512]{1,0:T(8,128)(2,1)S(1)}, u32[]{:S(2)}, u32[]{:S(2)}) collective-permute-start(bf16[656,512]{1,0:T(8,128)(2,1)S(1)} %get-tuple-element.180), channel_id=1, source_target_pairs={{0,1},{1,2},{2,3},{3,0},{4,5},{5,6},{6,7},{7,4},{8,9},{9,10},{10,1... | collective-permute-start | bytes 2015240 | tf_op jit(solution)/shard_map/ppermute | solution.py:643
  46.0 12.7 %collective-permute-start.5 = (bf16[656,256]{1,0:T(8,128)(2,1)}, bf16[656,256]{1,0:T(8,128)(2,1)}, u32[]{:S(2)}, u32[]{:S(2)}) collective-permute-start(bf16[656,256]{1,0:T(8,128)(2,1)} %slice.531), channel_id=1, source_target_pairs={{1,0},{2,1},{3,2},{0,3},{5,4},{6,5},{7,6},{4,7},{9,8},{10,9},{11,1... | collective-permute-start | bytes 1007624 | tf_op jit(solution)/shard_map/ppermute | solution.py:649
  51.0 14.0 %collective-permute-start.4 = (bf16[656,256]{1,0:T(8,128)(2,1)}, bf16[656,256]{1,0:T(8,128)(2,1)}, u32[]{:S(2)}, u32[]{:S(2)}) collective-permute-start(bf16[656,256]{1,0:T(8,128)(2,1)} %slice.530), channel_id=1, source_target_pairs={{0,1},{1,2},{2,3},{3,0},{4,5},{5,6},{6,7},{7,4},{8,9},{9,10},{10,1... | collective-permute-start | bytes 1007624 | tf_op jit(solution)/shard_map/ppermute | solution.py:648
  100.2 15.7 %collective-permute-start.10 = (bf16[512,9472]{1,0:T(8,128)(2,1)}, bf16[512,9472]{1,0:T(8,128)(2,1)}, u32[]{:S(2)}, u32[]{:S(2)}) collective-permute-start(bf16[512,9472]{1,0:T(8,128)(2,1)} %all-gather.3.cloned.1.call-done.weight_own.gate_own.up_own), channel_id=1, source_target_pairs={{0,64},{64,0},{1,65},{65,1},{2,66},{66,2},{3,67},{67,3},{4,68},{68... | collective-permute-start | bytes 29097992 | tf_op jit(solution)/shard_map/ppermute | solution.py:31
  100.9 34.7 %collective-permute-start.11 = (bf16[656,512]{1,0:T(8,128)(2,1)}, bf16[656,512]{1,0:T(8,128)(2,1)}, u32[]{:S(2)}, u32[]{:S(2)}) collective-permute-start(bf16[656,512]{1,0:T(8,128)(2,1)} %get-tuple-element.83), channel_id=1, source_target_pairs={{0,1},{1,2},{2,3},{3,0},{4,5},{5,6},{6,7},{7,4},{8,9},{9,10},{10,1... | collective-permute-start | bytes 2015240 | tf_op jit(solution)/shard_map/ppermute | solution.py:643
  101.4 34.2 %collective-permute-start.12 = (bf16[656,512]{1,0:T(8,128)(2,1)}, bf16[656,512]{1,0:T(8,128)(2,1)}, u32[]{:S(2)}, u32[]{:S(2)}) collective-permute-start(bf16[656,512]{1,0:T(8,128)(2,1)} %get-tuple-element.83), channel_id=1, source_target_pairs={{1,0},{2,1},{3,2},{0,3},{5,4},{6,5},{7,6},{4,7},{9,8},{10,9},{11,1... | collective-permute-start | bytes 2015240 | tf_op jit(solution)/shard_map/ppermute | solution.py:643
  137.0 13.8 %collective-permute-start.14 = (bf16[656,256]{1,0:T(8,128)(2,1)S(1)}, bf16[656,256]{1,0:T(8,128)(2,1)S(1)}, u32[]{:S(2)}, u32[]{:S(2)}) collective-permute-start(bf16[656,256]{1,0:T(8,128)(2,1)S(1)} %slice.443), channel_id=1, source_target_pairs={{1,0},{2,1},{3,2},{0,3},{5,4},{6,5},{7,6},{4,7},{9,8},{10,9},{11,1... | collective-permute-start | bytes 1007624 | tf_op jit(solution)/shard_map/ppermute | solution.py:649
  140.0 13.7 %collective-permute-start.13 = (bf16[656,256]{1,0:T(8,128)(2,1)S(1)}, bf16[656,256]{1,0:T(8,128)(2,1)S(1)}, u32[]{:S(2)}, u32[]{:S(2)}) collective-permute-start(bf16[656,256]{1,0:T(8,128)(2,1)S(1)} %slice.442), channel_id=1, source_target_pairs={{0,1},{1,2},{2,3},{3,0},{4,5},{5,6},{6,7},{7,4},{8,9},{9,10},{10,1... | collective-permute-start | bytes 1007624 | tf_op jit(solution)/shard_map/ppermute | solution.py:648
  156.6 32.6 %collective-permute-start.15 = (bf16[2688,512]{1,0:T(8,128)(2,1)}, bf16[2688,512]{1,0:T(8,128)(2,1)}, u32[]{:S(2)}, u32[]{:S(2)}) collective-permute-start(bf16[2688,512]{1,0:T(8,128)(2,1)} %constant_dynamic-update-slice_fusion.16.down_own), channel_id=1, source_target_pairs={{0,64},{64,0},{1,65},{65,1},{2,66},{66,2},{3,67},{67,3},{4,68},{68... | collective-permute-start | bytes 8257544 | tf_op jit(solution)/shard_map/ppermute | solution.py:31
  158.8 10.1 %collective-permute-start.17 = (bf16[64,1024]{1,0:T(8,128)(2,1)S(1)}, bf16[64,1024]{1,0:T(8,128)(2,1)S(1)}, u32[]{:S(2)}, u32[]{:S(2)}) collective-permute-start(bf16[64,1024]{1,0:T(8,128)(2,1)S(1)} %get-tuple-element.291), channel_id=1, source_target_pairs={{4,0},{8,4},{12,8},{16,12},{20,16},{24,20},{28,24},{32,28},{36,32}... | collective-permute-start | bytes 393224 | tf_op jit(solution)/shard_map/ppermute | solution.py:172
  161.0 10.0 %collective-permute-start.16 = (bf16[64,1024]{1,0:T(8,128)(2,1)S(1)}, bf16[64,1024]{1,0:T(8,128)(2,1)S(1)}, u32[]{:S(2)}, u32[]{:S(2)}) collective-permute-start(bf16[64,1024]{1,0:T(8,128)(2,1)S(1)} %get-tuple-element.290), channel_id=1, source_target_pairs={{0,4},{4,8},{8,12},{12,16},{16,20},{20,24},{24,28},{28,32},{32,36}... | collective-permute-start | bytes 393224 | tf_op jit(solution)/shard_map/ppermute | solution.py:168
  191.5 7.6 %collective-permute-start.18 = (bf16[512,3072]{1,0:T(8,128)(2,1)S(1)}, bf16[512,3072]{1,0:T(8,128)(2,1)S(1)}, u32[]{:S(2)}, u32[]{:S(2)}) collective-permute-start(bf16[512,3072]{1,0:T(8,128)(2,1)S(1)} %slice.455), channel_id=1, source_target_pairs={{0,64},{64,0},{1,65},{65,1},{2,66},{66,2},{3,67},{67,3},{4,68},{68... | collective-permute-start | bytes 9437192 | tf_op jit(solution)/shard_map/ppermute | solution.py:31
  199.0 15.4 %collective-permute-start.20 = (bf16[512,9472]{1,0:T(8,128)(2,1)}, bf16[512,9472]{1,0:T(8,128)(2,1)}, u32[]{:S(2)}, u32[]{:S(2)}) collective-permute-start(bf16[512,9472]{1,0:T(8,128)(2,1)} %all-gather.5.cloned.1.call-done.weight_own.gate_own.up_own), channel_id=1, source_target_pairs={{0,64},{64,0},{1,65},{65,1},{2,66},{66,2},{3,67},{67,3},{4,68},{68... | collective-permute-start | bytes 29097992 | tf_op jit(solution)/shard_map/ppermute | solution.py:31
  244.5 212.6 %reduce-scatter.3.cloned.1.call-start = ((), (), s32[]{:S(2)}) async-start(), calls=%async_computation.4 | async-start | bytes 13647872 | tf_op jit(solution)/shard_map/reduce_scatter | solution.py:416
  256.1 14.7 %collective-permute-start.26 = (bf16[64,2048]{1,0:T(8,128)(2,1)S(1)}, bf16[64,2048]{1,0:T(8,128)(2,1)S(1)}, u32[]{:S(2)}, u32[]{:S(2)}) collective-permute-start(bf16[64,2048]{1,0:T(8,128)(2,1)S(1)} %get-tuple-element.111), channel_id=1, source_target_pairs={{4,0},{8,4},{12,8},{16,12},{20,16},{24,20},{28,24},{32,28},{36,32}... | collective-permute-start | bytes 786440 | tf_op jit(solution)/shard_map/ppermute | solution.py:172
  259.5 13.0 %collective-permute-start.25 = (bf16[64,2048]{1,0:T(8,128)(2,1)S(1)}, bf16[64,2048]{1,0:T(8,128)(2,1)S(1)}, u32[]{:S(2)}, u32[]{:S(2)}) collective-permute-start(bf16[64,2048]{1,0:T(8,128)(2,1)S(1)} %get-tuple-element.110), channel_id=1, source_target_pairs={{0,4},{4,8},{8,12},{12,16},{16,20},{20,24},{24,28},{28,32},{32,36}... | collective-permute-start | bytes 786440 | tf_op jit(solution)/shard_map/ppermute | solution.py:168
  261.6 37.8 %collective-permute-start.29 = (bf16[3,128,1024]{2,1,0:T(8,128)(2,1)S(1)}, bf16[3,128,1024]{2,1,0:T(8,128)(2,1)S(1)}, u32[]{:S(2)}, u32[]{:S(2)}) collective-permute-start(bf16[3,128,1024]{2,1,0:T(8,128)(2,1)S(1)} %pad_maximum_fusion.7.refs_2_.refs_0_), channel_id=1, source_target_pairs={{0,64},{64,0},{1,65},{65,1},{2,66},{66,2},{3,67},{67,3},{4,68},{68... | collective-permute-start | bytes 2359304 | tf_op jit(solution)/shard_map/ppermute | solution.py:31
  262.5 36.8 %collective-permute-start.30 = (bf16[128,2688]{1,0:T(8,128)(2,1)S(1)}, bf16[128,2688]{1,0:T(8,128)(2,1)S(1)}, u32[]{:S(2)}, u32[]{:S(2)}) collective-permute-start(bf16[128,2688]{1,0:T(8,128)(2,1)S(1)} %copy-done.24), channel_id=1, source_target_pairs={{0,64},{64,0},{1,65},{65,1},{2,66},{66,2},{3,67},{67,3},{4,68},{68... | collective-permute-start | bytes 2064392 | tf_op jit(solution)/shard_map/ppermute | solution.py:31
  290.2 10.9 %collective-permute-start.27 = (bf16[128,3200]{1,0:T(8,128)(2,1)S(1)}, bf16[128,3200]{1,0:T(8,128)(2,1)S(1)}, u32[]{:S(2)}, u32[]{:S(2)}) collective-permute-start(bf16[128,3200]{1,0:T(8,128)(2,1)S(1)} %get-tuple-element.192), channel_id=1, source_target_pairs={{0,64},{64,0},{1,65},{65,1},{2,66},{66,2},{3,67},{67,3},{4,68},{68... | collective-permute-start | bytes 2457608 | tf_op jit(solution)/shard_map/ppermute | solution.py:31
  308.6 9.7 %collective-permute-start.32 = (bf16[64,2048]{1,0:T(8,128)(2,1)S(1)}, bf16[64,2048]{1,0:T(8,128)(2,1)S(1)}, u32[]{:S(2)}, u32[]{:S(2)}) collective-permute-start(bf16[64,2048]{1,0:T(8,128)(2,1)S(1)} %get-tuple-element.125), channel_id=1, source_target_pairs={{4,0},{8,4},{12,8},{16,12},{20,16},{24,20},{28,24},{32,28},{36,32}... | collective-permute-start | bytes 786440 | tf_op jit(solution)/shard_map/ppermute | solution.py:172
  310.5 10.3 %collective-permute-start.31 = (bf16[64,2048]{1,0:T(8,128)(2,1)S(1)}, bf16[64,2048]{1,0:T(8,128)(2,1)S(1)}, u32[]{:S(2)}, u32[]{:S(2)}) collective-permute-start(bf16[64,2048]{1,0:T(8,128)(2,1)S(1)} %get-tuple-element.124), channel_id=1, source_target_pairs={{0,4},{4,8},{8,12},{12,16},{16,20},{20,24},{24,28},{28,32},{32,36}... | collective-permute-start | bytes 786440 | tf_op jit(solution)/shard_map/ppermute | solution.py:168
  321.9 8.4 %collective-permute-start.33 = (bf16[128,2048]{1,0:T(8,128)(2,1)S(1)}, bf16[128,2048]{1,0:T(8,128)(2,1)S(1)}, u32[]{:S(2)}, u32[]{:S(2)}) collective-permute-start(bf16[128,2048]{1,0:T(8,128)(2,1)S(1)} %get-tuple-element.206), channel_id=1, source_target_pairs={{0,64},{64,0},{1,65},{65,1},{2,66},{66,2},{3,67},{67,3},{4,68},{68... | collective-permute-start | bytes 1572872 | tf_op jit(solution)/shard_map/ppermute | solution.py:31
  350.4 56.0 %collective-permute-start.49 = (bf16[16,16,2048]{2,1,0:T(8,128)(2,1)}, bf16[16,16,2048]{2,1,0:T(8,128)(2,1)}, u32[]{:S(2)}, u32[]{:S(2)}) collective-permute-start(bf16[16,16,2048]{2,1,0:T(8,128)(2,1)} %get-tuple-element.186), channel_id=1, source_target_pairs={{0,3},{1,0},{2,1},{3,2},{4,7},{5,4},{6,5},{7,6},{8,11},{9,8},{10,9... | collective-permute-start | bytes 3145736 | tf_op jit(solution)/shard_map/ppermute | solution.py:571
  353.0 59.8 %collective-permute-start.48 = (bf16[16,16,2048]{2,1,0:T(8,128)(2,1)}, bf16[16,16,2048]{2,1,0:T(8,128)(2,1)}, u32[]{:S(2)}, u32[]{:S(2)}) collective-permute-start(bf16[16,16,2048]{2,1,0:T(8,128)(2,1)} %get-tuple-element.187), channel_id=1, source_target_pairs={{0,2},{1,3},{2,0},{3,1},{4,6},{5,7},{6,4},{7,5},{8,10},{9,11},{10,... | collective-permute-start | bytes 3145736 | tf_op jit(solution)/shard_map/ppermute | solution.py:571
  353.1 61.7 %collective-permute-start.47 = (bf16[16,16,2048]{2,1,0:T(8,128)(2,1)}, bf16[16,16,2048]{2,1,0:T(8,128)(2,1)}, u32[]{:S(2)}, u32[]{:S(2)}) collective-permute-start(bf16[16,16,2048]{2,1,0:T(8,128)(2,1)} %get-tuple-element.185), channel_id=1, source_target_pairs={{0,1},{1,2},{2,3},{3,0},{4,5},{5,6},{6,7},{7,4},{8,9},{9,10},{10,1... | collective-permute-start | bytes 3145736 | tf_op jit(solution)/shard_map/ppermute | solution.py:571
  360.4 40.2 %collective-permute-start.40 = (bf16[16,16,128]{2,1,0:T(8,128)(2,1)S(1)}, bf16[16,16,128]{2,1,0:T(8,128)(2,1)S(1)}, u32[]{:S(2)}, u32[]{:S(2)}) collective-permute-start(bf16[16,16,128]{2,1,0:T(8,128)(2,1)S(1)} %get-tuple-element.254), channel_id=1, source_target_pairs={{0,3},{1,0},{2,1},{3,2},{4,7},{5,4},{6,5},{7,6},{8,11},{9,8},{10,9... | collective-permute-start | bytes 196616 | tf_op jit(solution)/shard_map/ppermute | solution.py:571
  362.3 40.1 %collective-permute-start.39 = (bf16[16,16,128]{2,1,0:T(8,128)(2,1)S(1)}, bf16[16,16,128]{2,1,0:T(8,128)(2,1)S(1)}, u32[]{:S(2)}, u32[]{:S(2)}) collective-permute-start(bf16[16,16,128]{2,1,0:T(8,128)(2,1)S(1)} %get-tuple-element.255), channel_id=1, source_target_pairs={{0,2},{1,3},{2,0},{3,1},{4,6},{5,7},{6,4},{7,5},{8,10},{9,11},{10,... | collective-permute-start | bytes 196616 | tf_op jit(solution)/shard_map/ppermute | solution.py:571
  402.4 75.4 %collective-permute-start.34 = (f32[128,1024]{1,0:T(8,128)S(1)}, f32[128,1024]{1,0:T(8,128)S(1)}, u32[]{:S(2)}, u32[]{:S(2)}) collective-permute-start(f32[128,1024]{1,0:T(8,128)S(1)} %get-tuple-element.169), channel_id=1, source_target_pairs={{0,64},{64,0},{1,65},{65,1},{2,66},{66,2},{3,67},{67,3},{4,68},{68... | collective-permute-start | bytes 1572872 | tf_op jit(solution)/shard_map/ppermute | solution.py:31
  406.3 11.5 %collective-permute-start.43 = (bf16[4,16,128]{2,1,0:T(8,128)(2,1)S(1)}, bf16[4,16,128]{2,1,0:T(8,128)(2,1)S(1)}, u32[]{:S(2)}, u32[]{:S(2)}) collective-permute-start(bf16[4,16,128]{2,1,0:T(8,128)(2,1)S(1)} %get-tuple-element.317), channel_id=1, source_target_pairs={{0,12},{4,0},{8,4},{12,8},{16,28},{20,16},{24,20},{28,24},{32,44},... | collective-permute-start | bytes 49160 | tf_op jit(solution)/shard_map/ppermute | solution.py:571
  406.4 12.6 %collective-permute-start.42 = (bf16[4,16,128]{2,1,0:T(8,128)(2,1)S(1)}, bf16[4,16,128]{2,1,0:T(8,128)(2,1)S(1)}, u32[]{:S(2)}, u32[]{:S(2)}) collective-permute-start(bf16[4,16,128]{2,1,0:T(8,128)(2,1)S(1)} %get-tuple-element.318), channel_id=1, source_target_pairs={{0,8},{4,12},{8,0},{12,4},{16,24},{20,28},{24,16},{28,20},{32,40},... | collective-permute-start | bytes 49160 | tf_op jit(solution)/shard_map/ppermute | solution.py:571
  412.8 7.8 %collective-permute-start.41 = (bf16[4,16,128]{2,1,0:T(8,128)(2,1)S(1)}, bf16[4,16,128]{2,1,0:T(8,128)(2,1)S(1)}, u32[]{:S(2)}, u32[]{:S(2)}) collective-permute-start(bf16[4,16,128]{2,1,0:T(8,128)(2,1)S(1)} %get-tuple-element.316), channel_id=1, source_target_pairs={{0,4},{4,8},{8,12},{12,0},{16,20},{20,24},{24,28},{28,16},{32,36},... | collective-permute-start | bytes 49160 | tf_op jit(solution)/shard_map/ppermute | solution.py:571
  417.7 12.5 %collective-permute-start.52 = (bf16[4,16,2048]{2,1,0:T(8,128)(2,1)S(1)}, bf16[4,16,2048]{2,1,0:T(8,128)(2,1)S(1)}, u32[]{:S(2)}, u32[]{:S(2)}) collective-permute-start(bf16[4,16,2048]{2,1,0:T(8,128)(2,1)S(1)} %get-tuple-element.202), channel_id=1, source_target_pairs={{0,12},{4,0},{8,4},{12,8},{16,28},{20,16},{24,20},{28,24},{32,44},... | collective-permute-start | bytes 786440 | tf_op jit(solution)/shard_map/ppermute | solution.py:571
  417.8 23.7 %collective-permute-start.51 = (bf16[4,16,2048]{2,1,0:T(8,128)(2,1)S(1)}, bf16[4,16,2048]{2,1,0:T(8,128)(2,1)S(1)}, u32[]{:S(2)}, u32[]{:S(2)}) collective-permute-start(bf16[4,16,2048]{2,1,0:T(8,128)(2,1)S(1)} %get-tuple-element.203), channel_id=1, source_target_pairs={{0,8},{4,12},{8,0},{12,4},{16,24},{20,28},{24,16},{28,20},{32,40},... | collective-permute-start | bytes 786440 | tf_op jit(solution)/shard_map/ppermute | solution.py:571
  419.0 25.7 %collective-permute-start.50 = (bf16[4,16,2048]{2,1,0:T(8,128)(2,1)S(1)}, bf16[4,16,2048]{2,1,0:T(8,128)(2,1)S(1)}, u32[]{:S(2)}, u32[]{:S(2)}) collective-permute-start(bf16[4,16,2048]{2,1,0:T(8,128)(2,1)S(1)} %get-tuple-element.201), channel_id=1, source_target_pairs={{0,4},{4,8},{8,12},{12,0},{16,20},{20,24},{24,28},{28,16},{32,36},... | collective-permute-start | bytes 786440 | tf_op jit(solution)/shard_map/ppermute | solution.py:571
  420.6 25.5 %collective-permute-start.46 = (bf16[16,128]{1,0:T(8,128)(2,1)S(1)}, bf16[16,128]{1,0:T(8,128)(2,1)S(1)}, u32[]{:S(2)}, u32[]{:S(2)}) collective-permute-start(bf16[16,128]{1,0:T(8,128)(2,1)S(1)} %get-tuple-element.320), channel_id=1, source_target_pairs={{0,48},{4,52},{8,56},{12,60},{16,0},{20,4},{24,8},{28,12},{32,16},... | collective-permute-start | bytes 12296 | tf_op jit(solution)/shard_map/ppermute | solution.py:571
  430.2 17.7 %collective-permute-start.45 = (bf16[16,128]{1,0:T(8,128)(2,1)S(1)}, bf16[16,128]{1,0:T(8,128)(2,1)S(1)}, u32[]{:S(2)}, u32[]{:S(2)}) collective-permute-start(bf16[16,128]{1,0:T(8,128)(2,1)S(1)} %get-tuple-element.321), channel_id=1, source_target_pairs={{0,32},{4,36},{8,40},{12,44},{16,48},{20,52},{24,56},{28,60},{32,0... | collective-permute-start | bytes 12296 | tf_op jit(solution)/shard_map/ppermute | solution.py:571
  441.5 6.6 %collective-permute-start.44 = (bf16[16,128]{1,0:T(8,128)(2,1)S(1)}, bf16[16,128]{1,0:T(8,128)(2,1)S(1)}, u32[]{:S(2)}, u32[]{:S(2)}) collective-permute-start(bf16[16,128]{1,0:T(8,128)(2,1)S(1)} %get-tuple-element.319), channel_id=1, source_target_pairs={{0,16},{4,20},{8,24},{12,28},{16,32},{20,36},{24,40},{28,44},{32,4... | collective-permute-start | bytes 12296 | tf_op jit(solution)/shard_map/ppermute | solution.py:571
  456.5 7.1 %collective-permute-start.56 = (bf16[16,4224]{1,0:T(8,128)(2,1)}, bf16[16,4224]{1,0:T(8,128)(2,1)}, u32[]{:S(2)}, u32[]{:S(2)}) collective-permute-start(bf16[16,4224]{1,0:T(8,128)(2,1)} %get-tuple-element.211), channel_id=1, source_target_pairs={{0,1},{1,2},{2,3},{3,0},{4,5},{5,6},{6,7},{7,4},{8,9},{9,10},{10,1... | collective-permute-start | bytes 405512 | tf_op jit(solution)/shard_map/ppermute | solution.py:554
  458.3 10.1 %collective-permute-start.37 = (bf16[16,6272]{1,0:T(8,128)(2,1)S(1)}, bf16[16,6272]{1,0:T(8,128)(2,1)S(1)}, u32[]{:S(2)}, u32[]{:S(2)}) collective-permute-start(bf16[16,6272]{1,0:T(8,128)(2,1)S(1)} %get-tuple-element.209), channel_id=1, source_target_pairs={{0,3},{1,0},{2,1},{3,2},{4,7},{5,4},{6,5},{7,6},{8,11},{9,8},{10,9... | collective-permute-start | bytes 602120 | tf_op jit(solution)/shard_map/ppermute | solution.py:554
  460.4 8.0 %collective-permute-start.36 = (bf16[16,6272]{1,0:T(8,128)(2,1)S(1)}, bf16[16,6272]{1,0:T(8,128)(2,1)S(1)}, u32[]{:S(2)}, u32[]{:S(2)}) collective-permute-start(bf16[16,6272]{1,0:T(8,128)(2,1)S(1)} %get-tuple-element.210), channel_id=1, source_target_pairs={{0,2},{1,3},{2,0},{3,1},{4,6},{5,7},{6,4},{7,5},{8,10},{9,11},{10,... | collective-permute-start | bytes 602120 | tf_op jit(solution)/shard_map/ppermute | solution.py:554
  462.3 9.9 %collective-permute-start.35 = (bf16[16,6272]{1,0:T(8,128)(2,1)S(1)}, bf16[16,6272]{1,0:T(8,128)(2,1)S(1)}, u32[]{:S(2)}, u32[]{:S(2)}) collective-permute-start(bf16[16,6272]{1,0:T(8,128)(2,1)S(1)} %get-tuple-element.208), channel_id=1, source_target_pairs={{0,1},{1,2},{2,3},{3,0},{4,5},{5,6},{6,7},{7,4},{8,9},{9,10},{10,1... | collective-permute-start | bytes 602120 | tf_op jit(solution)/shard_map/ppermute | solution.py:554
  473.4 7.4 %collective-permute-start.59 = (f32[16,6400]{1,0:T(8,128)S(1)}, f32[16,6400]{1,0:T(8,128)S(1)}, u32[]{:S(2)}, u32[]{:S(2)}) collective-permute-start(f32[16,6400]{1,0:T(8,128)S(1)} %fusion.30), channel_id=1, source_target_pairs={{0,64},{64,0},{1,65},{65,1},{2,66},{66,2},{3,67},{67,3},{4,68},{68... | collective-permute-start | bytes 1228808 | tf_op jit(solution)/shard_map/ppermute | solution.py:31
  (72 other events, 623.0 us)
Sparse Core Ops, SparseCore 0:
  12.7 87.4 all-gather.2
  103.5 85.6 all-gather.4
  244.6 91.0 reduce-scatter.4
  339.5 104.5 reduce-scatter.2

commit v2 on v1

--- a/solution.py
+++ b/solution.py
@@ -421,8 +421,7 @@
 
 
 def weight_grads(name, items, grads, total, product=None, base=None):
-    count, width = items[0][0].shape[1:]
-    block = 256
+    count, width, block = (grads[0][0].shape[0], HEADS * HEAD_DIM, 256)
     in_specs, args = ([], [])
     for acts, got, member, *_ in items:
         for array in (acts, got):
@@ -712,8 +711,7 @@
     attn_cols, out_cols, down_cols = (qkv_width // 2, half, ROW_GROUPS * half)
     hidden_end = FF_PAD + down_cols
     second_at = attn_cols + out_cols
-    side_at = out_cols + down_cols
-    hidden_at = second_at + attn_cols
+    hidden_at = 2 * second_at
     total = hidden_at + FF_PAD
 
     def attn_items(kept, which, at):
@@ -744,16 +742,13 @@
     late_grads, side_grads = ([], [])
 
     def make_joint(hidden_pair):
-        items, product = hidden_items(kept0, 1, hidden_at, out_cols)
-        qkv_item, out_item = attn_items(kept1, 0, 0)
+        items, product = hidden_items(kept0, 1, hidden_at, 0)
         pairs = [attn_pair1, hidden_pair]
-        late_grads.append(
-            weight_grads("joint_grads", [qkv_item[:-1] + (second_at,)] + items, pairs, total)[0]
-        )
+        items = attn_items(kept1, 0, second_at) + items
+        late_grads.append(weight_grads("joint_grads", items, pairs, total)[0])
+        product = (*product[:2], 0, *product[3:])
         side_grads.append(
-            functools.partial(
-                weight_grads, "side_grads", [out_item[:-1] + (0,)], pairs, side_at, product
-            )
+            functools.partial(weight_grads, "side_grads", [], [hidden_pair], down_cols, product)
         )
         return (hidden_pair[1], attn_pair1[1], *kept0[-1])
 
@@ -782,18 +777,19 @@
     section_outputs = placed(middle, final)
     section_input_grads = placed(grads0, grads1)
 
-    early_total, late_total = (summed_over_w(early, w_place), summed_over_w(late, w_place))
+    late, early_total, side_total, gain_part, section_outputs, section_input_grads = (
+        lax.optimization_barrier(
+            (
+                late, summed_over_w(early, w_place), side_total, gain_part, section_outputs,
+                section_input_grads,
+            )
+        )
+    )
+    late_total = summed_over_w(late, w_place)
     of_first = jnp.concatenate(
-        [
-            late_total[:, :second_at], gain_part, late_total[:, hidden_at:],
-            side_total[:, out_cols:],
-        ],
-        axis=1,
-    )
-    of_second = jnp.concatenate(
-        [late_total[:, second_at:hidden_at], side_total[:, :out_cols], gain_part, early_total],
-        axis=1,
-    )
+        [late_total[:, :second_at], gain_part, late_total[:, hidden_at:], side_total], axis=1
+    )
+    of_second = jnp.concatenate([late_total[:, second_at:hidden_at], gain_part, early_total], axis=1)
     mine, got = (by_core(of_first, of_second), swapped(by_core(of_second, of_first)))
     low, high = (by_core(mine, got), by_core(got, mine))
     hidden_at = second_at + 128

time: 502 us -> 488 us (0.972)
  the two profiles are of different devices: /device:TPU:3 before, /device:TPU:1 now
where the time goes in v2:
time: 488 us; the launch traced here: 479 us
  waiting for transfers between devices  213 us (44%)
  Pallas kernels  92.9 us (19%)
  starting transfers between devices  82.5 us (17%)
  local copies, waits for them, and re-layouts  33.5 us (7%)
  other arithmetic  30.1 us (6%)
  between operations  15.7 us (3%)
  matrix products  10.8 us (2%)
    pallas_call x12, Pallas kernels, grid_call(): pl.pallas_call(kernel, grid_spec=pltpu.PrefetchScalarGridSpec(num_scalar_...  73.8 us
    all_gather x2, waiting for transfers between devices, gathered(): return lax.all_gather(piece, ('wshard', 'seq'), axis=0, tiled=True)  47.4 us
    ppermute x18, waiting for transfers between devices, phase(): lax.ppermute(part(step), axis, route(step)).astype(jnp.float32)  39.3 us
    ppermute x20, waiting for transfers between devices, swapped(): return lax.ppermute(array, 'section', SWAP)  33.5 us
    ppermute x18, starting transfers between devices, phase(): lax.ppermute(part(step), axis, route(step)).astype(jnp.float32)  27.3 us
    ppermute x4, waiting for transfers between devices, to_next(): return lax.ppermute(array, 'seq', [(i, i + 1) for i in range(SEQ_DEV - 1)])  19.5 us
    ppermute x20, starting transfers between devices, swapped(): return lax.ppermute(array, 'section', SWAP)  17.6 us
    ppermute x4, waiting for transfers between devices, to_previous(): return lax.ppermute(array, 'seq', [(i + 1, i) for i in range(SEQ_DEV - 1)])  16.3 us
  transfers between devices with their start and end apart: 64, of which 36 were waited for; matrix products, arithmetic and copies ran while one was open for 11% of the time, Pallas kernels for 15%

profile of v2, /device:TPU:1, one launch (start us, length us, event | category | flops | bytes accessed | tf_op | source)
XLA Modules:
  0.0 478.7 jit_solution(10502683478873204710)
XLA Ops:
  16.7 3.2 collective-permute-start.8
  22.4 3.8 collective-permute-done.9
  27.3 2.7 constant_dynamic-update-slice_fusion.21
  33.8 15.2 %collective-permute-done.3 = bf16[656,512]{1,0:T(8,128)(2,1)S(1)} collective-permute-done((bf16[656,512]{1,0:T(8,128)(2,1)S(1)}, bf16[656,512]{1,0:T(8,128)(2,1)S(1)}, u32[]{:S(2)}, u32[]{:S(2)}) %collective-permute-start.3) | collective-permute-done | bytes 671776 | tf_op jit(solution)/shard_map/ppermute | solution.py:642
  52.2 2.7 collective-permute-start.5
  56.1 9.5 %collective-permute-done.4 = bf16[656,256]{1,0:T(8,128)(2,1)} collective-permute-done((bf16[656,256]{1,0:T(8,128)(2,1)}, bf16[656,256]{1,0:T(8,128)(2,1)}, u32[]{:S(2)}, u32[]{:S(2)}) %collective-permute-start.4) | collective-permute-done | bytes 335904 | tf_op jit(solution)/shard_map/ppermute | solution.py:647
  68.1 4.7 collective-permute-done.6.down_other
  72.9 27.8 %all-gather.3.cloned.1.call-done.weight_own.gate_own.up_own = bf16[512,9472]{1,0:T(8,128)(2,1)} async-done(((bf16[8,9472]{1,0:T(8,128)(2,1)}), bf16[512,9472]{1,0:T(8,128)(2,1)}) %all-gather.3.cloned.1.call-update) | async-done | bytes 9699344 | tf_op jit(solution)/shard_map/all_gather | solution.py:631
  105.4 10.9 %collective-permute-done.10.weight_other.gate_other.up_other = bf16[512,9472]{1,0:T(8,128)(2,1)} collective-permute-done((bf16[512,9472]{1,0:T(8,128)(2,1)}, bf16[512,9472]{1,0:T(8,128)(2,1)}, u32[]{:S(2)}, u32[]{:S(2)}) %collective-permute-start.10) | collective-permute-done | bytes 9699360 | tf_op jit(solution)/shard_map/ppermute | solution.py:31
  116.3 4.7 qkv.2
  121.1 2.9 attend.2
  128.5 8.1 %hidden.2 = (f32[128,2688]{1,0:T(8,128)S(1)}, f32[128,2688]{1,0:T(8,128)S(1)}, bf16[128,2688]{1,0:T(8,128)(2,1)S(1)}, f32[128,1024]{1,0:T(8,128)S(1)}) custom-call(s32[1]{0:T(128)} %bitcast.20.first, bf16[128,512]{1,0:T(8,128)(2,1)S(1)} %get-tuple-element.304.own, bf16[128,512]{1,0:T(8,128)(2,1)S(1)} %get-tuple-element.303.other, ...), custom_call_target="tpu_custom_call" | custom-call | tf_op jit(solution)/shard_map/hidden/pallas_call | solution.py:181
  139.6 2.7 collective-permute-start.15
  146.9 6.1 %collective-permute-done.14 = bf16[656,256]{1,0:T(8,128)(2,1)S(1)} collective-permute-done((bf16[656,256]{1,0:T(8,128)(2,1)S(1)}, bf16[656,256]{1,0:T(8,128)(2,1)S(1)}, u32[]{:S(2)}, u32[]{:S(2)}) %collective-permute-start.14) | collective-permute-done | bytes 335904 | tf_op jit(solution)/shard_map/ppermute | solution.py:647
  158.1 3.1 collective-permute-start.17
  162.5 4.6 collective-permute-done.17
  167.2 4.1 collective-permute-done.18
  171.3 19.7 %all-gather.5.cloned.1.call-done.weight_own.gate_own.up_own = bf16[512,9472]{1,0:T(8,128)(2,1)} async-done(((bf16[8,9472]{1,0:T(8,128)(2,1)}), bf16[512,9472]{1,0:T(8,128)(2,1)}) %all-gather.5.cloned.1.call-update) | async-done | bytes 9699344 | tf_op jit(solution)/shard_map/all_gather | solution.py:631
  195.3 5.4 %collective-permute-done.20 = bf16[512,1024]{1,0:T(8,128)(2,1)S(1)} collective-permute-done((bf16[512,1024]{1,0:T(8,128)(2,1)S(1)}, bf16[512,1024]{1,0:T(8,128)(2,1)S(1)}, u32[]{:S(2)}, u32[]{:S(2)}) %collective-permute-start.20) | collective-permute-done | bytes 1048608 | tf_op jit(solution)/shard_map/ppermute | solution.py:31
  201.5 4.8 %qkv.3 = bf16[256,3072]{1,0:T(8,128)(2,1)S(1)} custom-call(bf16[256,512]{1,0:T(8,128)(2,1)S(1)} %get-tuple-element.231.own, bf16[256,512]{1,0:T(8,128)(2,1)S(1)} %get-tuple-element.230.other, bf16[512,9472]{1,0:T(8,128)(2,1)} %all-gather.5.cloned.1.call-done.weight_own.gate_own.up_own, bf16[512,3072]{1,0:T(8,128)(2,1)S(1)} %collective-permute-done.19.weight_other), custom_call_target="tpu_custom_call" | custom-call | tf_op jit(solution)/shard_map/qkv/pallas_call | solution.py:181
  206.4 2.9 attend.3
  212.0 4.2 collective-permute-done.21.gate_other.up_other
  216.2 8.0 %hidden.3 = (f32[128,2688]{1,0:T(8,128)S(1)}, f32[128,2688]{1,0:T(8,128)S(1)}, bf16[128,2688]{1,0:T(8,128)(2,1)S(1)}, f32[128,1024]{1,0:T(8,128)S(1)}) custom-call(s32[1]{0:T(128)} %bitcast.20.first, bf16[128,512]{1,0:T(8,128)(2,1)S(1)} %get-tuple-element.284.own, bf16[128,512]{1,0:T(8,128)(2,1)S(1)} %get-tuple-element.283.other, ...), custom_call_target="tpu_custom_call" | custom-call | tf_op jit(solution)/shard_map/hidden/pallas_call | solution.py:181
  225.0 9.6 %hidden_back.2 = (bf16[128,2688]{1,0:T(8,128)(2,1)S(1)}, bf16[128,2688]{1,0:T(8,128)(2,1)S(1)}, f32[128,1024]{1,0:T(8,128)S(1)}) custom-call(s32[1]{0:T(128)} %bitcast.20.first, bf16[128,512]{1,0:T(8,128)(2,1)S(1)} %get-tuple-element.278.grad_own, bf16[128,512]{1,0:T(8,128)(2,1)S(1)} %get-tuple-element.279.grad_other, ...), custom_call_target="tpu_custom_call" | custom-call | tf_op jit(solution)/shard_map/hidden_back/pallas_call | solution.py:181
  239.4 5.9 %hidden_grads.1 = (bf16[1024,4224]{1,0:T(8,128)(2,1)}, f32[8,128]{1,0:T(8,128)S(1)}) custom-call(bf16[3,128,1024]{2,1,0:T(8,128)(2,1)S(1)} %pad_maximum_fusion.7.refs_0_.refs_2_, bf16[3,128,1024]{2,1,0:T(8,128)(2,1)S(1)} %collective-permute-done.22.refs_1_.refs_3_, bf16[128,3200]{1,0:T(8,128)(2,1)S(1)} %get-tuple-element.206.refs_2_, ...), custom_call_target="tpu_custom_call" | custom-call | tf_op jit(solution)/shard_map/hidden_grads/pallas_call | solution.py:181
  252.4 5.8 %attend_back.2 = (bf16[128,1024]{1,0:T(8,128)(2,1)S(1)}, f32[128,2048]{1,0:T(8,128)S(1)}, bf16[64,2048]{1,0:T(8,128)(2,1)S(1)}, bf16[64,2048]{1,0:T(8,128)(2,1)S(1)}) custom-call(s32[128,1]{1,0:T(8,128)S(1)} %copy.35.query_seg, s32[1,256]{1,0:T(1,128)S(1)} %bitcast.162, bf16[256,3072]{1,0:T(8,128)(2,1)S(1)} %qkv.3, f32[128,1024]{1,0:T(8,128)S(1)} %copy-done.22, ...), custom_call_target="tpu_custom_call" | custom-call | tf_op jit(solution)/shard_map/attend_back/pallas_call | solution.py:152
  262.1 9.4 %collective-permute-done.25 = bf16[64,2048]{1,0:T(8,128)(2,1)S(1)} collective-permute-done((bf16[64,2048]{1,0:T(8,128)(2,1)S(1)}, bf16[64,2048]{1,0:T(8,128)(2,1)S(1)}, u32[]{:S(2)}, u32[]{:S(2)}) %collective-permute-start.25) | collective-permute-done | bytes 262176 | tf_op jit(solution)/shard_map/ppermute | solution.py:168
  271.5 3.8 collective-permute-done.26
  277.4 5.1 %qkv_back.2 = f32[128,1024]{1,0:T(8,128)S(1)} custom-call(s32[1]{0:T(128)} %bitcast.20.first, bf16[128,3072]{1,0:T(8,128)(2,1)S(1)} %pad_maximum_fusion.grad, bf16[512,9472]{1,0:T(8,128)(2,1)} %all-gather.5.cloned.1.call-done.weight_own.gate_own.up_own, bf16[512,3072]{1,0:T(8,128)(2,1)S(1)} %copy-done.4), custom_call_target="tpu_custom_call" | custom-call | tf_op jit(solution)/shard_map/qkv_back/pallas_call | solution.py:181
  284.5 9.8 %hidden_back.3 = (bf16[128,2688]{1,0:T(8,128)(2,1)S(1)}, bf16[128,2688]{1,0:T(8,128)(2,1)S(1)}, f32[128,1024]{1,0:T(8,128)S(1)}) custom-call(s32[1]{0:T(128)} %bitcast.20.first, bf16[128,512]{1,0:T(8,128)(2,1)S(1)} %get-tuple-element.272.grad_own, bf16[128,512]{1,0:T(8,128)(2,1)S(1)} %get-tuple-element.273.grad_other, f32[128,2688]{1,0:T(8,128)S(1)} %copy-done.14, ...), custom_call_target="tpu_custom_call" | custom-call | tf_op jit(solution)/shard_map/hidden_back/pallas_call | solution.py:181
  301.3 7.4 %attend_back.3 = (bf16[128,1024]{1,0:T(8,128)(2,1)S(1)}, f32[128,2048]{1,0:T(8,128)S(1)}, bf16[64,2048]{1,0:T(8,128)(2,1)S(1)}, bf16[64,2048]{1,0:T(8,128)(2,1)S(1)}) custom-call(s32[128,1]{1,0:T(8,128)S(1)} %copy.35.query_seg, s32[1,256]{1,0:T(1,128)S(1)} %bitcast.163, bf16[256,3072]{1,0:T(8,128)(2,1)} %copy-done, f32[128,1024]{1,0:T(8,128)S(1)} %copy-done.24, ...), custom_call_target="tpu_custom_call" | custom-call | tf_op jit(solution)/shard_map/attend_back/pallas_call | solution.py:152
  308.8 2.7 collective-permute-start.30
  312.9 4.3 collective-permute-done.30
  317.2 4.5 collective-permute-done.31
  324.3 6.7 %joint_grads.1 = (bf16[1024,6784]{1,0:T(8,128)(2,1)}, f32[8,128]{1,0:T(8,128)}) custom-call(bf16[3,128,1024]{2,1,0:T(8,128)(2,1)S(1)} %copy-done.2, bf16[3,128,1024]{2,1,0:T(8,128)(2,1)S(1)} %copy-done.6, bf16[3,128,1024]{2,1,0:T(8,128)(2,1)S(1)} %copy-done.2, bf16[3,128,1024]{2,1,0:T(8,128)(2,1)S(1)} %copy-done.6, ...), custom_call_target="tpu_custom_call" | custom-call | tf_op jit(solution)/shard_map/joint_grads/pallas_call | solution.py:181
  331.0 3.7 attn_grads.1
  346.2 2.7 collective-permute-start.37
  350.1 6.0 %qkv_back.3 = f32[128,1024]{1,0:T(8,128)S(1)} custom-call(s32[1]{0:T(128)} %bitcast.20.first, bf16[128,3072]{1,0:T(8,128)(2,1)S(1)} %pad_maximum_fusion.1.grad, bf16[512,9472]{1,0:T(8,128)(2,1)} %all-gather.3.cloned.1.call-done.weight_own.gate_own.up_own, bf16[512,9472]{1,0:T(8,128)(2,1)} %collective-permute-done.10.weight_other.gate_other.up_other, ...), custom_call_target="tpu_custom_call" | custom-call | tf_op jit(solution)/shard_map/qkv_back/pallas_call | solution.py:181
  359.5 5.9 %collective-permute-done.36 = bf16[16,16,1536]{2,1,0:T(8,128)(2,1)S(1)} collective-permute-done((bf16[16,16,1536]{2,1,0:T(8,128)(2,1)}, bf16[16,16,1536]{2,1,0:T(8,128)(2,1)S(1)}, u32[]{:S(2)}, u32[]{:S(2)}) %collective-permute-start.36) | collective-permute-done | bytes 786464 | tf_op jit(solution)/shard_map/ppermute | solution.py:570
  366.8 16.5 %collective-permute-done.37 = bf16[16,16,1536]{2,1,0:T(8,128)(2,1)S(1)} collective-permute-done((bf16[16,16,1536]{2,1,0:T(8,128)(2,1)}, bf16[16,16,1536]{2,1,0:T(8,128)(2,1)S(1)}, u32[]{:S(2)}, u32[]{:S(2)}) %collective-permute-start.37) | collective-permute-done | bytes 786464 | tf_op jit(solution)/shard_map/ppermute | solution.py:570
  386.9 5.4 %collective-permute-start.48 = (bf16[4,16,128]{2,1,0:T(8,128)(2,1)S(1)}, bf16[4,16,128]{2,1,0:T(8,128)(2,1)S(1)}, u32[]{:S(2)}, u32[]{:S(2)}) collective-permute-start(bf16[4,16,128]{2,1,0:T(8,128)(2,1)S(1)} %get-tuple-element.330), channel_id=1, source_target_pairs={{0,4},{4,8},{8,12},{12,0},{16,20},{20,24},{24,28},{28,16},{32,36},... | collective-permute-start | bytes 49160 | tf_op jit(solution)/shard_map/ppermute | solution.py:570
  392.3 5.6 %collective-permute-start.49 = (bf16[4,16,128]{2,1,0:T(8,128)(2,1)S(1)}, bf16[4,16,128]{2,1,0:T(8,128)(2,1)S(1)}, u32[]{:S(2)}, u32[]{:S(2)}) collective-permute-start(bf16[4,16,128]{2,1,0:T(8,128)(2,1)S(1)} %get-tuple-element.332), channel_id=1, source_target_pairs={{0,8},{4,12},{8,0},{12,4},{16,24},{20,28},{24,16},{28,20},{32,40},... | collective-permute-start | bytes 49160 | tf_op jit(solution)/shard_map/ppermute | solution.py:570
  402.8 6.7 %collective-permute-done.39 = bf16[4,16,1536]{2,1,0:T(8,128)(2,1)S(1)} collective-permute-done((bf16[4,16,1536]{2,1,0:T(8,128)(2,1)S(1)}, bf16[4,16,1536]{2,1,0:T(8,128)(2,1)S(1)}, u32[]{:S(2)}, u32[]{:S(2)}) %collective-permute-start.39) | collective-permute-done | bytes 196640 | tf_op jit(solution)/shard_map/ppermute | solution.py:570
  409.6 6.9 %collective-permute-done.40 = bf16[4,16,1536]{2,1,0:T(8,128)(2,1)S(1)} collective-permute-done((bf16[4,16,1536]{2,1,0:T(8,128)(2,1)S(1)}, bf16[4,16,1536]{2,1,0:T(8,128)(2,1)S(1)}, u32[]{:S(2)}, u32[]{:S(2)}) %collective-permute-start.40) | collective-permute-done | bytes 196640 | tf_op jit(solution)/shard_map/ppermute | solution.py:570
  425.6 2.6 collective-permute-start.34
  433.1 15.9 %reduce-scatter.3.cloned.1.call-done = bf16[64,6784]{1,0:T(8,128)(2,1)} async-done(((bf16[1024,6784]{1,0:T(8,128)(2,1)}), bf16[64,6784]{1,0:T(8,128)(2,1)}) %reduce-scatter.3.cloned.1.call-update) | async-done | bytes 868368 | tf_op jit(solution)/shard_map/reduce_scatter | solution.py:416
  451.7 2.5 collective-permute-start.57
  457.7 5.7 %collective-permute-done.57 = bf16[16,6784]{1,0:T(8,128)(2,1)S(1)} collective-permute-done((bf16[16,6784]{1,0:T(8,128)(2,1)S(1)}, bf16[16,6784]{1,0:T(8,128)(2,1)S(1)}, u32[]{:S(2)}, u32[]{:S(2)}) %collective-permute-start.57) | collective-permute-done | bytes 217120 | tf_op jit(solution)/shard_map/ppermute | solution.py:553
  (364 shorter events, 139.9 us)
Async XLA Ops:
  7.2 93.5 %all-gather.3.cloned.1.call-start = ((), (), s32[]{:S(2)}) async-start(), calls=%async_computation.2 | async-start | bytes 9850880 | tf_op jit(solution)/shard_map/all_gather | solution.py:631
  13.3 177.6 %all-gather.5.cloned.1.call-start = ((), (), s32[]{:S(2)}) async-start(), calls=%async_computation.3 | async-start | bytes 9850880 | tf_op jit(solution)/shard_map/all_gather | solution.py:631
  13.5 13.7 %collective-permute-start.1 = (bf16[656,512]{1,0:T(8,128)(2,1)S(1)}, bf16[656,512]{1,0:T(8,128)(2,1)}, u32[]{:S(2)}, u32[]{:S(2)}) collective-permute-start(bf16[656,512]{1,0:T(8,128)(2,1)S(1)} %select_bitcast_fusion), channel_id=1, source_target_pairs={{0,64},{64,0},{1,65},{65,1},{2,66},{66,2},{3,67},{67,3},{4,68},{68... | collective-permute-start | bytes 2015240 | tf_op jit(solution)/shard_map/ppermute | solution.py:31
  16.7 5.7 %collective-permute-start.8 = (bf16[64,1024]{1,0:T(8,128)(2,1)S(1)}, bf16[64,1024]{1,0:T(8,128)(2,1)S(1)}, u32[]{:S(2)}, u32[]{:S(2)}) collective-permute-start(bf16[64,1024]{1,0:T(8,128)(2,1)S(1)} %get-tuple-element.321), channel_id=1, source_target_pairs={{0,4},{4,8},{8,12},{12,16},{16,20},{20,24},{24,28},{28,32},{32,36}... | collective-permute-start | bytes 393224 | tf_op jit(solution)/shard_map/ppermute | solution.py:168
  19.9 6.3 %collective-permute-start.9 = (bf16[64,1024]{1,0:T(8,128)(2,1)S(1)}, bf16[64,1024]{1,0:T(8,128)(2,1)S(1)}, u32[]{:S(2)}, u32[]{:S(2)}) collective-permute-start(bf16[64,1024]{1,0:T(8,128)(2,1)S(1)} %get-tuple-element.322), channel_id=1, source_target_pairs={{4,0},{8,4},{12,8},{16,12},{20,16},{24,20},{28,24},{32,28},{36,32}... | collective-permute-start | bytes 393224 | tf_op jit(solution)/shard_map/ppermute | solution.py:172
  27.1 396.8 %reduce-scatter.5.cloned.1.call-start = ((), (), s32[]{:S(2)}) async-start(), calls=%async_computation.5 | async-start | bytes 9191424 | tf_op jit(solution)/shard_map/reduce_scatter | solution.py:416
  30.0 19.0 %collective-permute-start.3 = (bf16[656,512]{1,0:T(8,128)(2,1)S(1)}, bf16[656,512]{1,0:T(8,128)(2,1)S(1)}, u32[]{:S(2)}, u32[]{:S(2)}) collective-permute-start(bf16[656,512]{1,0:T(8,128)(2,1)S(1)} %get-tuple-element.196), channel_id=1, source_target_pairs={{0,1},{1,2},{2,3},{3,0},{4,5},{5,6},{6,7},{7,4},{8,9},{9,10},{10,1... | collective-permute-start | bytes 2015240 | tf_op jit(solution)/shard_map/ppermute | solution.py:642
  31.7 19.0 %collective-permute-start.2 = (bf16[656,512]{1,0:T(8,128)(2,1)S(1)}, bf16[656,512]{1,0:T(8,128)(2,1)S(1)}, u32[]{:S(2)}, u32[]{:S(2)}) collective-permute-start(bf16[656,512]{1,0:T(8,128)(2,1)S(1)} %get-tuple-element.196), channel_id=1, source_target_pairs={{1,0},{2,1},{3,2},{0,3},{5,4},{6,5},{7,6},{4,7},{9,8},{10,9},{11,1... | collective-permute-start | bytes 2015240 | tf_op jit(solution)/shard_map/ppermute | solution.py:642
  50.6 15.0 %collective-permute-start.4 = (bf16[656,256]{1,0:T(8,128)(2,1)}, bf16[656,256]{1,0:T(8,128)(2,1)}, u32[]{:S(2)}, u32[]{:S(2)}) collective-permute-start(bf16[656,256]{1,0:T(8,128)(2,1)} %slice.522), channel_id=1, source_target_pairs={{0,1},{1,2},{2,3},{3,0},{4,5},{5,6},{6,7},{7,4},{8,9},{9,10},{10,1... | collective-permute-start | bytes 1007624 | tf_op jit(solution)/shard_map/ppermute | solution.py:647
  52.2 13.4 %collective-permute-start.5 = (bf16[656,256]{1,0:T(8,128)(2,1)}, bf16[656,256]{1,0:T(8,128)(2,1)}, u32[]{:S(2)}, u32[]{:S(2)}) collective-permute-start(bf16[656,256]{1,0:T(8,128)(2,1)} %slice.523), channel_id=1, source_target_pairs={{1,0},{2,1},{3,2},{0,3},{5,4},{6,5},{7,6},{4,7},{9,8},{10,9},{11,1... | collective-permute-start | bytes 1007624 | tf_op jit(solution)/shard_map/ppermute | solution.py:648
  66.8 6.1 %collective-permute-start.6 = (bf16[2688,512]{1,0:T(8,128)(2,1)S(1)}, bf16[2688,512]{1,0:T(8,128)(2,1)}, u32[]{:S(2)}, u32[]{:S(2)}) collective-permute-start(bf16[2688,512]{1,0:T(8,128)(2,1)S(1)} %constant_dynamic-update-slice_fusion.19.down_own), channel_id=1, source_target_pairs={{0,64},{64,0},{1,65},{65,1},{2,66},{66,2},{3,67},{67,3},{4,68},{68... | collective-permute-start | bytes 8257544 | tf_op jit(solution)/shard_map/ppermute | solution.py:31
  100.7 15.7 %collective-permute-start.10 = (bf16[512,9472]{1,0:T(8,128)(2,1)}, bf16[512,9472]{1,0:T(8,128)(2,1)}, u32[]{:S(2)}, u32[]{:S(2)}) collective-permute-start(bf16[512,9472]{1,0:T(8,128)(2,1)} %all-gather.3.cloned.1.call-done.weight_own.gate_own.up_own), channel_id=1, source_target_pairs={{0,64},{64,0},{1,65},{65,1},{2,66},{66,2},{3,67},{67,3},{4,68},{68... | collective-permute-start | bytes 29097992 | tf_op jit(solution)/shard_map/ppermute | solution.py:31
  101.3 35.3 %collective-permute-start.12 = (bf16[656,512]{1,0:T(8,128)(2,1)}, bf16[656,512]{1,0:T(8,128)(2,1)}, u32[]{:S(2)}, u32[]{:S(2)}) collective-permute-start(bf16[656,512]{1,0:T(8,128)(2,1)} %get-tuple-element.91), channel_id=1, source_target_pairs={{0,1},{1,2},{2,3},{3,0},{4,5},{5,6},{6,7},{7,4},{8,9},{9,10},{10,1... | collective-permute-start | bytes 2015240 | tf_op jit(solution)/shard_map/ppermute | solution.py:642
  101.9 34.7 %collective-permute-start.13 = (bf16[656,512]{1,0:T(8,128)(2,1)}, bf16[656,512]{1,0:T(8,128)(2,1)}, u32[]{:S(2)}, u32[]{:S(2)}) collective-permute-start(bf16[656,512]{1,0:T(8,128)(2,1)} %get-tuple-element.91), channel_id=1, source_target_pairs={{1,0},{2,1},{3,2},{0,3},{5,4},{6,5},{7,6},{4,7},{9,8},{10,9},{11,1... | collective-permute-start | bytes 2015240 | tf_op jit(solution)/shard_map/ppermute | solution.py:642
  138.0 15.0 %collective-permute-start.14 = (bf16[656,256]{1,0:T(8,128)(2,1)S(1)}, bf16[656,256]{1,0:T(8,128)(2,1)S(1)}, u32[]{:S(2)}, u32[]{:S(2)}) collective-permute-start(bf16[656,256]{1,0:T(8,128)(2,1)S(1)} %slice.438), channel_id=1, source_target_pairs={{0,1},{1,2},{2,3},{3,0},{4,5},{5,6},{6,7},{7,4},{8,9},{9,10},{10,1... | collective-permute-start | bytes 1007624 | tf_op jit(solution)/shard_map/ppermute | solution.py:647
  139.6 13.4 %collective-permute-start.15 = (bf16[656,256]{1,0:T(8,128)(2,1)S(1)}, bf16[656,256]{1,0:T(8,128)(2,1)S(1)}, u32[]{:S(2)}, u32[]{:S(2)}) collective-permute-start(bf16[656,256]{1,0:T(8,128)(2,1)S(1)} %slice.439), channel_id=1, source_target_pairs={{1,0},{2,1},{3,2},{0,3},{5,4},{6,5},{7,6},{4,7},{9,8},{10,9},{11,1... | collective-permute-start | bytes 1007624 | tf_op jit(solution)/shard_map/ppermute | solution.py:648
  155.9 35.1 %collective-permute-start.16 = (bf16[2688,512]{1,0:T(8,128)(2,1)}, bf16[2688,512]{1,0:T(8,128)(2,1)}, u32[]{:S(2)}, u32[]{:S(2)}) collective-permute-start(bf16[2688,512]{1,0:T(8,128)(2,1)} %constant_dynamic-update-slice_fusion.16.down_own), channel_id=1, source_target_pairs={{0,64},{64,0},{1,65},{65,1},{2,66},{66,2},{3,67},{67,3},{4,68},{68... | collective-permute-start | bytes 8257544 | tf_op jit(solution)/shard_map/ppermute | solution.py:31
  158.1 9.0 %collective-permute-start.17 = (bf16[64,1024]{1,0:T(8,128)(2,1)S(1)}, bf16[64,1024]{1,0:T(8,128)(2,1)S(1)}, u32[]{:S(2)}, u32[]{:S(2)}) collective-permute-start(bf16[64,1024]{1,0:T(8,128)(2,1)S(1)} %get-tuple-element.301), channel_id=1, source_target_pairs={{0,4},{4,8},{8,12},{12,16},{16,20},{20,24},{24,28},{28,32},{32,36}... | collective-permute-start | bytes 393224 | tf_op jit(solution)/shard_map/ppermute | solution.py:168
  161.2 10.0 %collective-permute-start.18 = (bf16[64,1024]{1,0:T(8,128)(2,1)S(1)}, bf16[64,1024]{1,0:T(8,128)(2,1)S(1)}, u32[]{:S(2)}, u32[]{:S(2)}) collective-permute-start(bf16[64,1024]{1,0:T(8,128)(2,1)S(1)} %get-tuple-element.302), channel_id=1, source_target_pairs={{4,0},{8,4},{12,8},{16,12},{20,16},{24,20},{28,24},{32,28},{36,32}... | collective-permute-start | bytes 393224 | tf_op jit(solution)/shard_map/ppermute | solution.py:172
  193.2 7.5 %collective-permute-start.19 = (bf16[512,3072]{1,0:T(8,128)(2,1)S(1)}, bf16[512,3072]{1,0:T(8,128)(2,1)S(1)}, u32[]{:S(2)}, u32[]{:S(2)}) collective-permute-start(bf16[512,3072]{1,0:T(8,128)(2,1)S(1)} %slice.451), channel_id=1, source_target_pairs={{0,64},{64,0},{1,65},{65,1},{2,66},{66,2},{3,67},{67,3},{4,68},{68... | collective-permute-start | bytes 9437192 | tf_op jit(solution)/shard_map/ppermute | solution.py:31
  200.7 15.4 %collective-permute-start.21 = (bf16[512,9472]{1,0:T(8,128)(2,1)}, bf16[512,9472]{1,0:T(8,128)(2,1)}, u32[]{:S(2)}, u32[]{:S(2)}) collective-permute-start(bf16[512,9472]{1,0:T(8,128)(2,1)} %all-gather.5.cloned.1.call-done.weight_own.gate_own.up_own), channel_id=1, source_target_pairs={{0,64},{64,0},{1,65},{65,1},{2,66},{66,2},{3,67},{67,3},{4,68},{68... | collective-permute-start | bytes 29097992 | tf_op jit(solution)/shard_map/ppermute | solution.py:31
  246.2 202.8 %reduce-scatter.3.cloned.1.call-start = ((), (), s32[]{:S(2)}) async-start(), calls=%async_computation.4 | async-start | bytes 14761984 | tf_op jit(solution)/shard_map/reduce_scatter | solution.py:416
  246.3 55.0 %collective-permute-start.29 = (bf16[128,2688]{1,0:T(8,128)(2,1)}, bf16[128,2688]{1,0:T(8,128)(2,1)S(1)}, u32[]{:S(2)}, u32[]{:S(2)}) collective-permute-start(bf16[128,2688]{1,0:T(8,128)(2,1)} %copy-done.19), channel_id=1, source_target_pairs={{0,64},{64,0},{1,65},{65,1},{2,66},{66,2},{3,67},{67,3},{4,68},{68... | collective-permute-start | bytes 2064392 | tf_op jit(solution)/shard_map/ppermute | solution.py:31
  258.2 13.2 %collective-permute-start.25 = (bf16[64,2048]{1,0:T(8,128)(2,1)S(1)}, bf16[64,2048]{1,0:T(8,128)(2,1)S(1)}, u32[]{:S(2)}, u32[]{:S(2)}) collective-permute-start(bf16[64,2048]{1,0:T(8,128)(2,1)S(1)} %get-tuple-element.117), channel_id=1, source_target_pairs={{0,4},{4,8},{8,12},{12,16},{16,20},{20,24},{24,28},{28,32},{32,36}... | collective-permute-start | bytes 786440 | tf_op jit(solution)/shard_map/ppermute | solution.py:168
  260.1 15.2 %collective-permute-start.26 = (bf16[64,2048]{1,0:T(8,128)(2,1)S(1)}, bf16[64,2048]{1,0:T(8,128)(2,1)S(1)}, u32[]{:S(2)}, u32[]{:S(2)}) collective-permute-start(bf16[64,2048]{1,0:T(8,128)(2,1)S(1)} %get-tuple-element.118), channel_id=1, source_target_pairs={{4,0},{8,4},{12,8},{16,12},{20,16},{24,20},{28,24},{32,28},{36,32}... | collective-permute-start | bytes 786440 | tf_op jit(solution)/shard_map/ppermute | solution.py:172
  261.5 39.8 %collective-permute-start.11 = (bf16[3,128,1024]{2,1,0:T(8,128)(2,1)S(1)}, bf16[3,128,1024]{2,1,0:T(8,128)(2,1)S(1)}, u32[]{:S(2)}, u32[]{:S(2)}) collective-permute-start(bf16[3,128,1024]{2,1,0:T(8,128)(2,1)S(1)} %pad_maximum_fusion.6.refs_4_.refs_0_.refs_2_), channel_id=1, source_target_pairs={{0,64},{64,0},{1,65},{65,1},{2,66},{66,2},{3,67},{67,3},{4,68},{68... | collective-permute-start | bytes 2359304 | tf_op jit(solution)/shard_map/ppermute | solution.py:31
  275.7 25.6 %collective-permute-start.28 = (bf16[128,2048]{1,0:T(8,128)(2,1)S(1)}, bf16[128,2048]{1,0:T(8,128)(2,1)S(1)}, u32[]{:S(2)}, u32[]{:S(2)}) collective-permute-start(bf16[128,2048]{1,0:T(8,128)(2,1)S(1)} %get-tuple-element.214), channel_id=1, source_target_pairs={{0,64},{64,0},{1,65},{65,1},{2,66},{66,2},{3,67},{67,3},{4,68},{68... | collective-permute-start | bytes 1572872 | tf_op jit(solution)/shard_map/ppermute | solution.py:31
  294.6 6.7 %collective-permute-start.27 = (bf16[128,3200]{1,0:T(8,128)(2,1)S(1)}, bf16[128,3200]{1,0:T(8,128)(2,1)S(1)}, u32[]{:S(2)}, u32[]{:S(2)}) collective-permute-start(bf16[128,3200]{1,0:T(8,128)(2,1)S(1)} %get-tuple-element.204), channel_id=1, source_target_pairs={{0,64},{64,0},{1,65},{65,1},{2,66},{66,2},{3,67},{67,3},{4,68},{68... | collective-permute-start | bytes 2457608 | tf_op jit(solution)/shard_map/ppermute | solution.py:31
  308.8 8.4 %collective-permute-start.30 = (bf16[64,2048]{1,0:T(8,128)(2,1)S(1)}, bf16[64,2048]{1,0:T(8,128)(2,1)S(1)}, u32[]{:S(2)}, u32[]{:S(2)}) collective-permute-start(bf16[64,2048]{1,0:T(8,128)(2,1)S(1)} %get-tuple-element.128), channel_id=1, source_target_pairs={{0,4},{4,8},{8,12},{12,16},{16,20},{20,24},{24,28},{28,32},{32,36}... | collective-permute-start | bytes 786440 | tf_op jit(solution)/shard_map/ppermute | solution.py:168
  311.5 10.2 %collective-permute-start.31 = (bf16[64,2048]{1,0:T(8,128)(2,1)S(1)}, bf16[64,2048]{1,0:T(8,128)(2,1)S(1)}, u32[]{:S(2)}, u32[]{:S(2)}) collective-permute-start(bf16[64,2048]{1,0:T(8,128)(2,1)S(1)} %get-tuple-element.129), channel_id=1, source_target_pairs={{4,0},{8,4},{12,8},{16,12},{20,16},{24,20},{28,24},{32,28},{36,32}... | collective-permute-start | bytes 786440 | tf_op jit(solution)/shard_map/ppermute | solution.py:172
  322.1 8.9 %collective-permute-start.32 = (bf16[128,2048]{1,0:T(8,128)(2,1)S(1)}, bf16[128,2048]{1,0:T(8,128)(2,1)S(1)}, u32[]{:S(2)}, u32[]{:S(2)}) collective-permute-start(bf16[128,2048]{1,0:T(8,128)(2,1)S(1)} %get-tuple-element.215), channel_id=1, source_target_pairs={{0,64},{64,0},{1,65},{65,1},{2,66},{66,2},{3,67},{67,3},{4,68},{68... | collective-permute-start | bytes 1572872 | tf_op jit(solution)/shard_map/ppermute | solution.py:31
  344.9 20.5 %collective-permute-start.36 = (bf16[16,16,1536]{2,1,0:T(8,128)(2,1)}, bf16[16,16,1536]{2,1,0:T(8,128)(2,1)S(1)}, u32[]{:S(2)}, u32[]{:S(2)}) collective-permute-start(bf16[16,16,1536]{2,1,0:T(8,128)(2,1)} %get-tuple-element.197), channel_id=1, source_target_pairs={{0,1},{1,2},{2,3},{3,0},{4,5},{5,6},{6,7},{7,4},{8,9},{9,10},{10,1... | collective-permute-start | bytes 2359304 | tf_op jit(solution)/shard_map/ppermute | solution.py:570
  346.2 37.1 %collective-permute-start.37 = (bf16[16,16,1536]{2,1,0:T(8,128)(2,1)}, bf16[16,16,1536]{2,1,0:T(8,128)(2,1)S(1)}, u32[]{:S(2)}, u32[]{:S(2)}) collective-permute-start(bf16[16,16,1536]{2,1,0:T(8,128)(2,1)} %get-tuple-element.199), channel_id=1, source_target_pairs={{0,2},{1,3},{2,0},{3,1},{4,6},{5,7},{6,4},{7,5},{8,10},{9,11},{10,... | collective-permute-start | bytes 2359304 | tf_op jit(solution)/shard_map/ppermute | solution.py:570
  348.9 34.4 %collective-permute-start.38 = (bf16[16,16,1536]{2,1,0:T(8,128)(2,1)}, bf16[16,16,1536]{2,1,0:T(8,128)(2,1)}, u32[]{:S(2)}, u32[]{:S(2)}) collective-permute-start(bf16[16,16,1536]{2,1,0:T(8,128)(2,1)} %get-tuple-element.198), channel_id=1, source_target_pairs={{0,3},{1,0},{2,1},{3,2},{4,7},{5,4},{6,5},{7,6},{8,11},{9,8},{10,9... | collective-permute-start | bytes 2359304 | tf_op jit(solution)/shard_map/ppermute | solution.py:570
  357.4 65.3 %collective-permute-start.55 = (f32[128,1024]{1,0:T(8,128)}, f32[128,1024]{1,0:T(8,128)}, u32[]{:S(2)}, u32[]{:S(2)}) collective-permute-start(f32[128,1024]{1,0:T(8,128)} %get-tuple-element.181), channel_id=1, source_target_pairs={{0,64},{64,0},{1,65},{65,1},{2,66},{66,2},{3,67},{67,3},{4,68},{68... | collective-permute-start | bytes 1572872 | tf_op jit(solution)/shard_map/ppermute | solution.py:31
  358.8 26.5 %collective-permute-start.45 = (bf16[16,16,128]{2,1,0:T(8,128)(2,1)S(1)}, bf16[16,16,128]{2,1,0:T(8,128)(2,1)S(1)}, u32[]{:S(2)}, u32[]{:S(2)}) collective-permute-start(bf16[16,16,128]{2,1,0:T(8,128)(2,1)S(1)} %get-tuple-element.264), channel_id=1, source_target_pairs={{0,1},{1,2},{2,3},{3,0},{4,5},{5,6},{6,7},{7,4},{8,9},{9,10},{10,1... | collective-permute-start | bytes 196616 | tf_op jit(solution)/shard_map/ppermute | solution.py:570
  365.4 20.4 %collective-permute-start.46 = (bf16[16,16,128]{2,1,0:T(8,128)(2,1)S(1)}, bf16[16,16,128]{2,1,0:T(8,128)(2,1)S(1)}, u32[]{:S(2)}, u32[]{:S(2)}) collective-permute-start(bf16[16,16,128]{2,1,0:T(8,128)(2,1)S(1)} %get-tuple-element.266), channel_id=1, source_target_pairs={{0,2},{1,3},{2,0},{3,1},{4,6},{5,7},{6,4},{7,5},{8,10},{9,11},{10,... | collective-permute-start | bytes 196616 | tf_op jit(solution)/shard_map/ppermute | solution.py:570
  386.9 12.6 %collective-permute-start.48 = (bf16[4,16,128]{2,1,0:T(8,128)(2,1)S(1)}, bf16[4,16,128]{2,1,0:T(8,128)(2,1)S(1)}, u32[]{:S(2)}, u32[]{:S(2)}) collective-permute-start(bf16[4,16,128]{2,1,0:T(8,128)(2,1)S(1)} %get-tuple-element.330), channel_id=1, source_target_pairs={{0,4},{4,8},{8,12},{12,0},{16,20},{20,24},{24,28},{28,16},{32,36},... | collective-permute-start | bytes 49160 | tf_op jit(solution)/shard_map/ppermute | solution.py:570
  392.3 7.6 %collective-permute-start.49 = (bf16[4,16,128]{2,1,0:T(8,128)(2,1)S(1)}, bf16[4,16,128]{2,1,0:T(8,128)(2,1)S(1)}, u32[]{:S(2)}, u32[]{:S(2)}) collective-permute-start(bf16[4,16,128]{2,1,0:T(8,128)(2,1)S(1)} %get-tuple-element.332), channel_id=1, source_target_pairs={{0,8},{4,12},{8,0},{12,4},{16,24},{20,28},{24,16},{28,20},{32,40},... | collective-permute-start | bytes 49160 | tf_op jit(solution)/shard_map/ppermute | solution.py:570
  397.9 11.6 %collective-permute-start.39 = (bf16[4,16,1536]{2,1,0:T(8,128)(2,1)S(1)}, bf16[4,16,1536]{2,1,0:T(8,128)(2,1)S(1)}, u32[]{:S(2)}, u32[]{:S(2)}) collective-permute-start(bf16[4,16,1536]{2,1,0:T(8,128)(2,1)S(1)} %get-tuple-element.220), channel_id=1, source_target_pairs={{0,4},{4,8},{8,12},{12,0},{16,20},{20,24},{24,28},{28,16},{32,36},... | collective-permute-start | bytes 589832 | tf_op jit(solution)/shard_map/ppermute | solution.py:570
  399.5 17.0 %collective-permute-start.40 = (bf16[4,16,1536]{2,1,0:T(8,128)(2,1)S(1)}, bf16[4,16,1536]{2,1,0:T(8,128)(2,1)S(1)}, u32[]{:S(2)}, u32[]{:S(2)}) collective-permute-start(bf16[4,16,1536]{2,1,0:T(8,128)(2,1)S(1)} %get-tuple-element.222), channel_id=1, source_target_pairs={{0,8},{4,12},{8,0},{12,4},{16,24},{20,28},{24,16},{28,20},{32,40},... | collective-permute-start | bytes 589832 | tf_op jit(solution)/shard_map/ppermute | solution.py:570
  399.8 16.7 %collective-permute-start.41 = (bf16[4,16,1536]{2,1,0:T(8,128)(2,1)S(1)}, bf16[4,16,1536]{2,1,0:T(8,128)(2,1)S(1)}, u32[]{:S(2)}, u32[]{:S(2)}) collective-permute-start(bf16[4,16,1536]{2,1,0:T(8,128)(2,1)S(1)} %get-tuple-element.221), channel_id=1, source_target_pairs={{0,12},{4,0},{8,4},{12,8},{16,28},{20,16},{24,20},{28,24},{32,44},... | collective-permute-start | bytes 589832 | tf_op jit(solution)/shard_map/ppermute | solution.py:570
  402.0 16.2 %collective-permute-start.51 = (bf16[16,128]{1,0:T(8,128)(2,1)S(1)}, bf16[16,128]{1,0:T(8,128)(2,1)S(1)}, u32[]{:S(2)}, u32[]{:S(2)}) collective-permute-start(bf16[16,128]{1,0:T(8,128)(2,1)S(1)} %get-tuple-element.333), channel_id=1, source_target_pairs={{0,16},{4,20},{8,24},{12,28},{16,32},{20,36},{24,40},{28,44},{32,4... | collective-permute-start | bytes 12296 | tf_op jit(solution)/shard_map/ppermute | solution.py:570
  409.5 9.9 %collective-permute-start.52 = (bf16[16,128]{1,0:T(8,128)(2,1)S(1)}, bf16[16,128]{1,0:T(8,128)(2,1)S(1)}, u32[]{:S(2)}, u32[]{:S(2)}) collective-permute-start(bf16[16,128]{1,0:T(8,128)(2,1)S(1)} %get-tuple-element.335), channel_id=1, source_target_pairs={{0,32},{4,36},{8,40},{12,44},{16,48},{20,52},{24,56},{28,60},{32,0... | collective-permute-start | bytes 12296 | tf_op jit(solution)/shard_map/ppermute | solution.py:570
  425.6 6.5 %collective-permute-start.34 = (bf16[16,4224]{1,0:T(8,128)(2,1)S(1)}, bf16[16,4224]{1,0:T(8,128)(2,1)S(1)}, u32[]{:S(2)}, u32[]{:S(2)}) collective-permute-start(bf16[16,4224]{1,0:T(8,128)(2,1)S(1)} %get-tuple-element.225), channel_id=1, source_target_pairs={{0,2},{1,3},{2,0},{3,1},{4,6},{5,7},{6,4},{7,5},{8,10},{9,11},{10,... | collective-permute-start | bytes 405512 | tf_op jit(solution)/shard_map/ppermute | solution.py:553
  450.2 7.4 %collective-permute-start.56 = (bf16[16,6784]{1,0:T(8,128)(2,1)S(1)}, bf16[16,6784]{1,0:T(8,128)(2,1)S(1)}, u32[]{:S(2)}, u32[]{:S(2)}) collective-permute-start(bf16[16,6784]{1,0:T(8,128)(2,1)S(1)} %get-tuple-element.217), channel_id=1, source_target_pairs={{0,1},{1,2},{2,3},{3,0},{4,5},{5,6},{6,7},{7,4},{8,9},{9,10},{10,1... | collective-permute-start | bytes 651272 | tf_op jit(solution)/shard_map/ppermute | solution.py:553
  451.7 11.7 %collective-permute-start.57 = (bf16[16,6784]{1,0:T(8,128)(2,1)S(1)}, bf16[16,6784]{1,0:T(8,128)(2,1)S(1)}, u32[]{:S(2)}, u32[]{:S(2)}) collective-permute-start(bf16[16,6784]{1,0:T(8,128)(2,1)S(1)} %get-tuple-element.219), channel_id=1, source_target_pairs={{0,2},{1,3},{2,0},{3,1},{4,6},{5,7},{6,4},{7,5},{8,10},{9,11},{10,... | collective-permute-start | bytes 651272 | tf_op jit(solution)/shard_map/ppermute | solution.py:553
  454.3 9.1 %collective-permute-start.58 = (bf16[16,6784]{1,0:T(8,128)(2,1)S(1)}, bf16[16,6784]{1,0:T(8,128)(2,1)S(1)}, u32[]{:S(2)}, u32[]{:S(2)}) collective-permute-start(bf16[16,6784]{1,0:T(8,128)(2,1)S(1)} %get-tuple-element.218), channel_id=1, source_target_pairs={{0,3},{1,0},{2,1},{3,2},{4,7},{5,4},{6,5},{7,6},{8,11},{9,8},{10,9... | collective-permute-start | bytes 651272 | tf_op jit(solution)/shard_map/ppermute | solution.py:553
  (64 other events, 413.8 us)
Sparse Core Ops, SparseCore 0:
  13.5 87.1 all-gather.2
  104.0 86.9 all-gather.4
  246.3 90.5 reduce-scatter.4
  340.7 108.3 reduce-scatter.2
